TPU v7x, 256 devices: a whole 4x4x8 slice. The times are simulated.
256 devices in a mesh: hist: 32 (over x, z), head: 8 (over y, core).
Axes of the slice: x: 4, y: 4, z: 8, core: 2. Of those that a mesh axis runs over, the one named last changes fastest.
Arguments:
- queries: bfloat16 [3584, 5120], P('hist', 'head'), as said below
- cache_keys: bfloat16 [43008, 5120], P('hist', 'head'), as said below
- cache_values: bfloat16 [43008, 5120], P('hist', 'head'), may hold values from -6 to 6
- hist_lengths: int32 [32], P('hist'), may hold values from 336 to 1344, as said below
- frame_bounds: int32 [4], replicated, may hold values from 21504 to 43008, as said below
- latent: bfloat16 [384, 3, 96, 160], P('head', None, 'hist'), as said below
- norm_gain: float32 [384], P('head'), may hold values from 0.1 to 1.9
- conv_weight: bfloat16 [3, 3, 3, 384, 384], P(None, None, None, 'head'), may hold values from -0.0625 to 0.0625
- conv_bias: float32 [384], P('head'), may hold values from -3 to 3
Outputs:
- attention: bfloat16 [3584, 5120], P('hist', 'head')
- vae_out: bfloat16 [384, 96, 160], P('head', 'hist')
Inputs may be any that keep to these rules, and one draw needn't show every extreme that they name: `queries`: Real-valued query vectors. `cache_keys`: Real-valued key vectors. `hist_lengths`: some block is full and some block holds exactly 336 filled slots. `frame_bounds`: never falling from one span to the next; the last span sees all 43008 slots. `latent`: Real-valued features.
All inputs are finite; a program needn't handle non-finite values.
Results may differ from a plain program's by a relative error of at most 0.017.
Values may be sent and summed in bfloat16 or wider, within the bound.
No kernel may reach another device: no remote copies, remote signals or barrier semaphores. Data moves between devices by JAX's collectives and lax.ppermute only.
A program may use at most 128 MiB of HBM per device.

v0:
```python
import functools
import math

import jax
import jax.numpy as jnp
from jax import lax
from jax.experimental import pallas as pl
from jax.experimental.pallas import tpu as pltpu
from jax.sharding import PartitionSpec as P

HEAD_DIM = 128
CHANNELS = 384
NX = 4
NZ = 8

NEG = -1e30
LOG2E = math.log2(math.e)
norm_eps = 1e-06
VMEM = 56 << 20
SIZES = (640, 1024)

ALONG_X = [[x * NZ + z for x in range(NX)] for z in range(NZ)]
ALONG_Z = [[x * NZ + z for z in range(NZ)] for x in range(NX)]

vmem = pl.BlockSpec(memory_space=pltpu.VMEM)
smem = pl.BlockSpec(memory_space=pltpu.SMEM)


def hist_shift(dx):
    return [(x * NZ + z, ((x + dx) % NX) * NZ + z) for x in range(NX) for z in range(NZ)]


def dot(a, b, dims):
    return lax.dot_general(a, b, (dims, ((), ())), preferred_element_type=jnp.float32)


def cost(micros, nbytes):
    return pl.CostEstimate(
        flops=int(micros * 1.1e9), bytes_accessed=nbytes, transcendentals=0
    )


def pack_queries_kernel(q_ref, out, last):
    for i in range(NX):
        out[i] = q_ref[:, i * 128 : (i + 1) * 128]
    last[...] = q_ref[:, NX * 128 :]


def pack_queries(queries):
    rows = queries.shape[0]
    return pl.pallas_call(
        pack_queries_kernel,
        out_shape=[
            jax.ShapeDtypeStruct((NX, rows, 128), jnp.bfloat16),
            jax.ShapeDtypeStruct((rows, 128), jnp.bfloat16),
        ],
        cost_estimate=cost(1, 1 << 18),
        name="pack_q",
    )(queries)


def pack_cache_kernel(len_ref, k_ref, v_ref, *outs):
    x = lax.axis_index("hist") // NZ
    rows = k_ref.shape[0]
    length = len_ref[0]
    row = lax.broadcasted_iota(jnp.int32, (16, 256), 0)
    tail = jnp.where(row == 0, length // 64, jnp.where(row == 1, lax.rem(length, 64), 0))
    tail = tail.astype(jnp.float32).astype(jnp.bfloat16)
    for d, out in enumerate(outs):
        head = lax.rem(x + d, NX) if d < NX else NX
        cols = pl.ds(pl.multiple_of(head * 128, 128), 128)
        out[:rows, :128] = k_ref[:, cols]
        out[:rows, 128:] = v_ref[:, cols]
        out[rows:, :] = tail


def pack_cache(lengths, keys, values):
    rows = keys.shape[0]
    return pl.pallas_call(
        pack_cache_kernel,
        in_specs=[smem, vmem, vmem],
        out_shape=[jax.ShapeDtypeStruct((rows + 16, 256), jnp.bfloat16)] * (NX + 1),
        compiler_params=pltpu.CompilerParams(vmem_limit_bytes=VMEM),
        cost_estimate=cost(3, 7 << 20),
        name="pack_kv",
    )(lengths, keys, values)


def unit(q_of, n, group, k_of, v_of, limit, rows, acc_ref, l_ref, m_ref, c2):
    def step(low, count):
        row = lax.broadcasted_iota(jnp.int32, (count - low, 128), 0) + low
        seen = row < limit
        first = jnp.broadcast_to(k_of(0, 16).astype(jnp.float32)[:1, :], (count - low, 128))
        k = jnp.where(seen, k_of(low, count).astype(jnp.float32), first).astype(jnp.bfloat16)
        v = jnp.where(seen, v_of(low, count).astype(jnp.float32), 0.0).astype(jnp.bfloat16)
        one = jnp.where(seen, 1.0, 0.0).astype(jnp.bfloat16)
        v = jnp.concatenate([v, one], axis=1)
        if low:
            k = jnp.concatenate([k_of(0, low), k], axis=0)
            ahead = [v_of(0, low), jnp.ones((low, 128), jnp.bfloat16)]
            v = jnp.concatenate([jnp.concatenate(ahead, axis=1), v], axis=0)

        s = dot(q_of(0), k, ((1,), (1,)))
        for g in range(n):
            later = dot(q_of(g + 1), k, ((1,), (1,))) if g + 1 < n else None
            here = slice(g * group, (g + 1) * group)
            old = m_ref[here, :]
            new = jnp.maximum(old, jnp.max(s, axis=1, keepdims=True) * c2)
            p = jnp.exp2(s * c2 - new[:, :1]).astype(jnp.bfloat16)
            r = dot(p, v, ((1,), (0,)))
            a = jnp.exp2(old - new)
            acc_ref[here, :] = acc_ref[here, :] * a + r[:, :128]
            l_ref[here, :] = l_ref[here, :] * a + r[:, 128:]
            m_ref[here, :] = new
            s = later

    low = 0
    for size in SIZES + (rows,):
        pl.when((limit > low) & (limit <= size))(functools.partial(step, low, size))
        low = size


def three_parts(value):
    high = value.astype(jnp.bfloat16).astype(jnp.float32)
    rest = value - high
    mid = rest.astype(jnp.bfloat16).astype(jnp.float32)
    return [high, mid, rest - mid]


def attn_kernel(slots, part, rows, c2, bounds_ref, q_ref, *refs):
    own = slots == 2
    kv_refs, refs = refs[:NX], refs[NX:]
    count = NX
    if own:
        all_ref, refs = refs[0], refs[1:]
        kv_refs = kv_refs + tuple(all_ref.at[i] for i in range(NX))
        count = 2 * NX
    out, q_buf, kv, acc_ref, l_ref, m_ref, q_sem, kv_sems = refs
    copies = [pltpu.make_async_copy(q_ref, q_buf, q_sem)]
    for u, ref in enumerate(kv_refs):
        copies.append(pltpu.make_async_copy(ref, kv.at[u], kv_sems.at[u]))
    for c in copies:
        c.start()
    acc_ref[...] = jnp.zeros_like(acc_ref)
    l_ref[...] = jnp.zeros_like(l_ref)
    m_ref[...] = jnp.full_like(m_ref, NEG)
    h = lax.axis_index("hist")
    x, z = h // NZ, lax.rem(h, NZ)
    many = NZ // 2
    for c in copies:
        c.wait()

    def body(step, carry):
        if own:
            u, slot = step, step // NX
            block_x = jnp.where(slot == 0, lax.rem(x - u + NX, NX), u - NX)
            frame = x
        else:
            u, slot = step // slots, lax.rem(step, slots)
            block_x = lax.rem(x - u + NX, NX)
            frame = lax.rem(x + 1 + slot, NX)
        tail = kv[u, rows : rows + 16, :128].astype(jnp.float32)
        row = lax.broadcasted_iota(jnp.int32, (16, 128), 0)
        high = jnp.max(jnp.where(row == 0, tail, 0.0))
        low = jnp.max(jnp.where(row == 1, tail, 0.0))
        length = (high * 64.0 + low).astype(jnp.int32)
        at = pl.ds(pl.multiple_of(slot * part, 16), part)
        unit(
            lambda g: q_buf[g * many : (g + 1) * many, at, :].reshape(many * part, 128),
            2,
            many * part,
            lambda a, b: kv[u, a:b, :128],
            lambda a, b: kv[u, a:b, 128:],
            jnp.minimum(length, bounds_ref[frame] - (block_x * NZ + z) * rows),
            rows,
            acc_ref.at[slot],
            l_ref.at[slot],
            m_ref.at[slot],
            c2,
        )
        return carry

    lax.fori_loop(0, slots * NX, body, 0)
    lane = lax.broadcasted_iota(jnp.int32, (part, 128), 1)
    fill = jnp.zeros((128 - part, 128), jnp.float32)
    empty = jnp.zeros((10, 128), jnp.float32)
    for slot in range(slots):
        base = slot * (part + 16)
        for g in range(NZ):
            here = slice(g * part, (g + 1) * part)
            out[g, base : base + part, :] = acc_ref[slot, here, :].astype(jnp.bfloat16)
            table = jnp.where(lane == 0, m_ref[slot, here, :], l_ref[slot, here, :])
            flat = jnp.concatenate([table, fill], axis=0).T[:2, :]
            flat = jnp.concatenate(three_parts(flat) + [empty], axis=0)
            out[g, base + part : base + part + 16, :] = flat.astype(jnp.bfloat16)


def attn(bounds, queries, kvs, part, c2):
    rows = kvs[0].shape[0] - 16
    slots = queries.shape[1] // part
    count = NX * (len(kvs) - NX + 1)
    anys = pl.BlockSpec(memory_space=pl.ANY)
    return pl.pallas_call(
        functools.partial(attn_kernel, slots, part, rows, c2),
        out_shape=jax.ShapeDtypeStruct((NZ, slots * (part + 16), 128), jnp.bfloat16),
        in_specs=[smem, anys] + [anys] * len(kvs),
        out_specs=vmem,
        scratch_shapes=[
            pltpu.VMEM((NZ, slots * part, 128), jnp.bfloat16),
            pltpu.VMEM((count, rows + 16, 256), jnp.bfloat16),
        ]
        + [pltpu.VMEM((slots, NZ * part, 128), jnp.float32)] * 3
        + [pltpu.SemaphoreType.DMA, pltpu.SemaphoreType.DMA((count,))],
        compiler_params=pltpu.CompilerParams(vmem_limit_bytes=VMEM),
        cost_estimate=cost(8 * slots, 1 << 20),
        name="attn",
    )(bounds, queries, *kvs)


def stat(rows16, count, which):
    at = [k * count + which for k in range(3)]
    return sum(rows16[a : a + 1, :] for a in at)


def merge_z(ref, part, slot):
    base = slot * (part + 16)
    under = slice(base + part, base + part + 16)
    stats = [ref[s, under, :].astype(jnp.float32) for s in range(NZ)]
    tops = [stat(st, 2, 0) for st in stats]
    top = functools.reduce(jnp.maximum, tops)
    raw = [jnp.exp2(t - top) for t in tops]
    total = functools.reduce(jnp.add, [r * stat(st, 2, 1) for r, st in zip(raw, stats)])
    total = jnp.maximum(total, 1.0)
    fill = jnp.zeros((128 - NZ, 128), jnp.float32)
    table = jnp.concatenate([r / total for r in raw] + [fill], axis=0).T
    out = jnp.zeros((part, 128), jnp.float32)
    for s in range(NZ):
        out += table[:part, s : s + 1] * ref[s, base : base + part, :].astype(jnp.float32)
    return out.astype(jnp.bfloat16)


def merge_kernel(part, ref, *outs):
    for slot, out in enumerate(outs):
        out[...] = merge_z(ref, part, slot)


def merge(payload, part):
    return pl.pallas_call(
        functools.partial(merge_kernel, part),
        out_shape=[jax.ShapeDtypeStruct((part, 128), jnp.bfloat16)] * (NX - 1),
        cost_estimate=cost(2, 1 << 20),
        name="merge",
    )(payload)


def finish_kernel(part, ref, *refs):
    others, out = refs[: NX - 1], refs[NX - 1]
    x = lax.axis_index("hist") // NZ
    out[:, pl.ds(pl.multiple_of(x * 128, 128), 128)] = merge_z(ref, part, 0)
    out[:, NX * 128 :] = merge_z(ref, part, 1)
    for k, r in enumerate(others):
        head = lax.rem(x + NX - 1 - k, NX)
        out[:, pl.ds(pl.multiple_of(head * 128, 128), 128)] = r[...]


def finish(payload, others, part):
    return pl.pallas_call(
        functools.partial(finish_kernel, part),
        out_shape=jax.ShapeDtypeStruct((part, (NX + 1) * 128), jnp.bfloat16),
        cost_estimate=cost(2, 1 << 20),
        name="finish",
    )(payload, *others)


def exchange(value, axis, groups=None):
    return lax.all_to_all(value, axis, 0, 0, axis_index_groups=groups)


def to_all_z(value):
    return exchange(jnp.broadcast_to(value[None], (NZ,) + value.shape), "hist", ALONG_Z)


def attention_part(queries, keys, values, length, bounds, conv):
    part = queries.shape[0]
    c2 = HEAD_DIM ** (-0.5) * LOG2E
    x = lax.axis_index("hist") // NZ
    packed, last = pack_queries(queries)
    mine = exchange(packed, "hist", ALONG_X)
    keys, values, _ = lax.optimization_barrier((keys, values, packed))
    cache = pack_cache(length, keys, values)
    kvs = [lax.ppermute(cache[d], "hist", hist_shift(d)) for d in range(1, NX)]
    kvs = [cache[0]] + kvs
    mine, _ = lax.optimization_barrier((mine, cache[0]))
    order = lax.dynamic_slice_in_dim(jnp.concatenate([mine, mine]), x + 1, NX, 0)
    foreign = to_all_z(order[: NX - 1].reshape((NX - 1) * part, 128))
    terms = conv()
    kvs, terms, foreign = lax.optimization_barrier((kvs, terms, foreign))
    last_cache, own, _ = lax.optimization_barrier(
        (cache[NX], jnp.concatenate([order[NX - 1], last], axis=0), foreign)
    )
    own = to_all_z(own)
    every = lax.all_gather(last_cache, "hist", axis=0, axis_index_groups=ALONG_X)

    landed = exchange(attn(bounds, foreign, kvs, part, c2), "hist", ALONG_Z)
    landed_own = exchange(attn(bounds, own, kvs + [every], part, c2), "hist", ALONG_Z)
    others = [
        lax.ppermute(r, "hist", hist_shift(i + 1)) for i, r in enumerate(merge(landed, part))
    ]
    return finish(landed_own, others, part), terms


def once(fun, *args):
    shapes = jax.eval_shape(fun, *args)
    turns = 1 + lax.axis_index("hist") // lax.axis_size("hist")

    def body(_, carry):
        return lax.optimization_barrier((carry[0], fun(*carry[0])))

    return lax.fori_loop(0, turns, body, (args, jnp.zeros(shapes.shape, shapes.dtype)))[1]


def conv_terms(latent, norm_gain, conv_weight):
    channels, times, rows, width = latent.shape
    flat = latent.reshape(channels, times * rows * width)
    whole = lax.all_gather(flat, "head", axis=0, tiled=True)

    def activate(flat, whole, norm_gain):
        squares = jnp.sum(jnp.square(whole.astype(jnp.float32)), axis=0)
        scaled = (
            flat.astype(jnp.float32)
            * lax.rsqrt(squares / CHANNELS + norm_eps)[None]
            * norm_gain[:, None]
        )
        return jax.nn.silu(scaled).astype(jnp.bfloat16).reshape(latent.shape)

    act = once(activate, flat, whole, norm_gain)
    count = lax.axis_size("hist")
    forward = [(i, i + 1) for i in range(count - 1)]
    backward = [(b, a) for a, b in forward]
    low = lax.ppermute(act[:, :, -1:], "hist", forward)
    high = lax.ppermute(act[:, :, :1], "hist", backward)

    def multiply(low, act, high, conv_weight):
        padded = jnp.pad(
            jnp.concatenate([low, act, high], axis=2), ((0, 0), (0, 0), (0, 0), (1, 1))
        )
        windows = [
            padded[:, a, b : b + rows, e : e + width]
            for a in range(3)
            for b in range(3)
            for e in range(3)
        ]
        patches = jnp.concatenate(windows, axis=0)
        weight = conv_weight.reshape(27 * channels, conv_weight.shape[4])
        terms = jnp.einsum("kyx,ko->oyx", patches, weight, preferred_element_type=jnp.float32)
        return terms.astype(jnp.bfloat16).reshape(-1, rows * width)

    return once(multiply, low, act, high, conv_weight)


def conv_sum(terms, conv_bias, shape):
    total = lax.psum_scatter(terms, "head", scatter_dimension=0, tiled=True)
    out = (total.astype(jnp.float32) + conv_bias[:, None]).astype(jnp.bfloat16)
    return out.reshape(shape)


def on_device(
    queries,
    cache_keys,
    cache_values,
    hist_lengths,
    frame_bounds,
    latent,
    norm_gain,
    conv_weight,
    conv_bias,
):
    attention, terms = attention_part(
        queries,
        cache_keys,
        cache_values,
        hist_lengths,
        frame_bounds,
        lambda: conv_terms(latent, norm_gain, conv_weight),
    )
    shape = (latent.shape[0], latent.shape[2], latent.shape[3])
    return (attention, conv_sum(terms, conv_bias, shape))


def solution(mesh):
    placed = (
        P("hist", "head"),
        P("hist", "head"),
        P("hist", "head"),
        P("hist"),
        P(),
        P("head", None, "hist", None),
        P("head"),
        P(None, None, None, "head", None),
        P("head"),
    )
    return jax.shard_map(
        on_device,
        mesh=mesh,
        in_specs=placed,
        out_specs=(P("hist", "head"), P("head", "hist", None)),
        check_vma=False,
    )
```

profile of v0, /device:TPU:7, one launch (start us, length us, event | category | flops | bytes accessed | tf_op | source)
XLA Modules:
  0.0 155.9 jit_solution(3996536622847096623)
XLA Ops:
  9.2 1.6 %pack_q.1 = (bf16[4,112,128]{2,1,0:T(8,128)(2,1)}, bf16[112,128]{1,0:T(8,128)(2,1)}) custom-call(bf16[112,640]{1,0:T(8,128)(2,1)} %q_ref.1), custom_call_target="tpu_custom_call" | custom-call | flops 1100000000 | bytes 262144 | tf_op jit(solution)/shard_map/pack_q/pallas_call | solution.py:51
  10.8 4.2 %all-to-all-start = ((bf16[4,112,128]{2,1,0:T(8,128)(2,1)}), bf16[4,112,128]{2,1,0:T(8,128)(2,1)S(1)}, u32[]{:S(2)}, u32[]{:S(2)}) async-start(bf16[4,112,128]{2,1,0:T(8,128)(2,1)} %get-tuple-element.162), calls=%async_computation | async-start | bytes 229376 | tf_op jit(solution)/shard_map/all_to_all | solution.py:276
  15.6 4.3 %pack_kv.1 = (bf16[1360,256]{1,0:T(8,128)(2,1)}, bf16[1360,256]{1,0:T(8,128)(2,1)}, bf16[1360,256]{1,0:T(8,128)(2,1)}, bf16[1360,256]{1,0:T(8,128)(2,1)}, bf16[1360,256]{1,0:T(8,128)(2,1)}) custom-call(s32[1]{0:T(128)S(6)} %copy.49.len_ref, bf16[1344,640]{1,0:T(8,128)(2,1)} %k_ref, bf16[1344,640]{1,0:T(8,128)(2,1)} %v_ref), custom_call_target="tpu_custom_call" | custom-call | flops 3300000000 | bytes 7340032 | tf_op jit(solution)/shard_map/pack_kv/pallas_call | solution.py:79
  19.9 2.4 %collective-permute-start.1 = (bf16[1360,256]{1,0:T(8,128)(2,1)}, bf16[1360,256]{1,0:T(8,128)(2,1)}, u32[]{:S(2)}, u32[]{:S(2)}) collective-permute-start(bf16[1360,256]{1,0:T(8,128)(2,1)} %get-tuple-element.170), channel_id=1, source_target_pairs={{0,128},{8,136},{16,144},{24,152},{32,160},{40,168},{48,176},{56,1... | collective-permute-start | bytes 2088968 | tf_op jit(solution)/shard_map/ppermute | solution.py:291
  23.4 8.2 %all-to-all-start.1 = ((bf16[8,336,128]{2,1,0:T(8,128)(2,1)}), bf16[8,336,128]{2,1,0:T(8,128)(2,1)}, u32[]{:S(2)}, u32[]{:S(2)}) async-start(bf16[8,336,128]{2,1,0:T(8,128)(2,1)} %broadcast_in_dim.25), calls=%async_computation.1 | async-start | bytes 1376256 | tf_op jit(solution)/shard_map/all_to_all | solution.py:276
  31.6 7.8 %all-gather.4.cloned.1.call-done = bf16[384,1440]{1,0:T(8,128)(2,1)} async-done(((bf16[48,1440]{1,0:T(8,128)(2,1)}), bf16[384,1440]{1,0:T(8,128)(2,1)}) %all-gather.4.cloned.1.call-update) | async-done | bytes 1105936 | tf_op jit(solution)/shard_map/all_gather | solution.py:325
  40.2 2.7 %while.36 = (s32[]{:T(128)}, bf16[48,1440]{1,0:T(8,128)(2,1)S(1)}, bf16[384,1440]{1,0:T(8,128)(2,1)}, f32[48]{0:T(128)S(1)}, bf16[48,3,3,160]{3,2,1,0:T(4,128)(2,1)}, /*index=5*/s32[]{:T(128)}, s32[]{:T(128)}) while((s32[]{:T(128)}, bf16[48,1440]{1,0:T(8,128)(2,1)S(1)}, bf16[384,1440]{1,0:T(8,128)(2,1)}, f32[48]{0:T(128)S(1)}, ...), condition=%wide.region_2.3_spmd, body=%wide.region_0.2_spmd.sunk | while | flops 2213282 | bytes 1682189 | solution.py:319
  40.2 1.5 multiply_reduce_fusion.2
  44.2 3.2 %collective-permute-start.3 = (bf16[48,3,1,160]{0,3,2,1:T(8,128)(2,1)S(1)}, bf16[48,3,1,160]{0,3,2,1:T(8,128)(2,1)S(1)}, u32[]{:S(2)}, u32[]{:S(2)}) collective-permute-start(bf16[48,3,1,160]{0,3,2,1:T(8,128)(2,1)S(1)} %get-tuple-element.278), channel_id=1, source_target_pairs={{0,8},{8,16},{16,24},{24,32},{32,40},{40,48},{48,56},{56,64},{64,7... | collective-permute-start | bytes 138248 | tf_op jit(solution)/shard_map/ppermute | solution.py:340
  47.4 4.2 %collective-permute-start.4 = (bf16[48,3,1,160]{0,3,2,1:T(8,128)(2,1)S(1)}, bf16[48,3,1,160]{0,3,2,1:T(8,128)(2,1)S(1)}, u32[]{:S(2)}, u32[]{:S(2)}) collective-permute-start(bf16[48,3,1,160]{0,3,2,1:T(8,128)(2,1)S(1)} %get-tuple-element.277), channel_id=1, source_target_pairs={{8,0},{16,8},{24,16},{32,24},{40,32},{48,40},{56,48},{64,56},{72,6... | collective-permute-start | bytes 138248 | tf_op jit(solution)/shard_map/ppermute | solution.py:341
  51.6 2.7 %collective-permute-done.3 = bf16[48,3,1,160]{0,3,2,1:T(8,128)(2,1)S(1)} collective-permute-done((bf16[48,3,1,160]{0,3,2,1:T(8,128)(2,1)S(1)}, bf16[48,3,1,160]{0,3,2,1:T(8,128)(2,1)S(1)}, u32[]{:S(2)}, u32[]{:S(2)}) %collective-permute-start.3) | collective-permute-done | bytes 46112 | tf_op jit(solution)/shard_map/ppermute | solution.py:340
  55.2 9.8 %while.37 = (s32[]{:T(128)}, bf16[48,3,1,160]{0,3,2,1:T(8,128)(2,1)S(1)}, bf16[48,3,3,160]{0,3,2,1:T(8,128)(2,1)S(1)}, bf16[48,3,1,160]{0,3,2,1:T(8,128)(2,1)S(1...) while((s32[]{:T(128)}, ...), condition=%wide.region_4.5_spmd, body=%wide.region_3.4_spmd.sunk | while | flops 479341440 | bytes 9569173 | solution.py:319
  58.4 3.7 %concatenate.41 = bf16[1296,3,160]{0,2,1:T(8,128)(2,1)S(1)} concatenate(bf16[48,3,160]{0,2,1:T(8,128)(2,1)} %get-tuple-element.399, bf16[48,3,160]{0,2,1:T(8,128)(2,1)} %get-tuple-element.402, bf16[48,3,160]{0,2,1:T(8,128)(2,1)} %get-tuple-element.403, bf16[48,3,160]{0,2,1:T(8,128)(2,1)} %get-tuple-element.404, bf16[48,3,160]{0,2,1:T(8,128)(2,1)} %get-tuple-element.405, ...), dimensions={0} | concatenate | bytes 2488320 | tf_op jit(solution)/shard_map/while/body/concatenate | solution.py:353
  62.1 2.9 %convolution_convert_fusion.2 = bf16[3,160,384]{2,1,0:T(8,128)(2,1)} fusion(bf16[1296,3,160]{0,2,1:T(8,128)(2,1)S(1)} %concatenate.41, bf16[1296,384,1]{1,0,2:T(8,128)(2,1)} %bitcast.84), kind=kOutput, calls=%fused_computation.6.clone.1 | convolution fusion | flops 477941760 | bytes 2608128 | tf_op jit(solution)/shard_map/while/body/kyx,ko->oyx/dot_general | solution.py:355
  65.9 6.2 %all-to-all-start.2 = ((bf16[8,224,128]{2,1,0:T(8,128)(2,1)}), bf16[8,224,128]{2,1,0:T(8,128)(2,1)S(1)}, u32[]{:S(2)}, u32[]{:S(2)}) async-start(bf16[8,224,128]{2,1,0:T(8,128)(2,1)} %broadcast_in_dim.26), calls=%async_computation.2 | async-start | bytes 917504 | tf_op jit(solution)/shard_map/all_to_all | solution.py:276
  73.4 17.0 %attn.3 = bf16[8,384,128]{2,1,0:T(8,128)(2,1)} custom-call(s32[4]{0:T(128)} %bounds_ref.3, bf16[8,336,128]{2,1,0:T(8,128)(2,1)} %all-to-all-done.1.q_ref, bf16[1360,256]{1,0:T(8,128)(2,1)} %get-tuple-element.176.refs_0_, bf16[1360,256]{1,0:T(8,128)(2,1)} %collective-permute-done.refs_1_, bf16[1360,256]{1,0:T(8,128)(2,1)} %collective-permute-done.1.refs_2_, ...), custom_call_target="tpu_custom_call" | custom-call | flops 26400000000 | bytes 1048576 | tf_op jit(solution)/shard_map/attn/pallas_call | solution.py:203
  90.3 7.7 %all-to-all-start.4 = ((bf16[8,384,128]{2,1,0:T(8,128)(2,1)}), bf16[8,384,128]{2,1,0:T(8,128)(2,1)S(1)}, u32[]{:S(2)}, u32[]{:S(2)}) async-start(bf16[8,384,128]{2,1,0:T(8,128)(2,1)} %attn.3), calls=%async_computation.4 | async-start | bytes 1572864 | tf_op jit(solution)/shard_map/all_to_all | solution.py:276
  98.1 4.7 %all-gather.6.cloned.1.call-done = bf16[5440,256]{1,0:T(8,128)(2,1)} async-done(((bf16[1360,256]{1,0:T(8,128)(2,1)}), bf16[5440,256]{1,0:T(8,128)(2,1)}) %all-gather.6.cloned.1.call-update) | async-done | bytes 2785296 | tf_op jit(solution)/shard_map/all_gather | solution.py:302
  102.8 16.8 %attn.2 = bf16[8,256,128]{2,1,0:T(8,128)(2,1)} custom-call(s32[4]{0:T(128)} %bounds_ref.3, bf16[8,224,128]{2,1,0:T(8,128)(2,1)} %copy-done.4, bf16[1360,256]{1,0:T(8,128)(2,1)} %get-tuple-element.176.refs_0_, bf16[1360,256]{1,0:T(8,128)(2,1)} %collective-permute-done.refs_1_, bf16[1360,256]{1,0:T(8,128)(2,1)} %collective-permute-done.1.refs_2_, ...), custom_call_target="tpu_custom_call" | custom-call | flops 17600000000 | bytes 1048576 | tf_op jit(solution)/shard_map/attn/pallas_call | solution.py:203
  119.7 8.8 %all-to-all-start.3 = ((bf16[8,256,128]{2,1,0:T(8,128)(2,1)}), bf16[8,256,128]{2,1,0:T(8,128)(2,1)S(1)}, u32[]{:S(2)}, u32[]{:S(2)}) async-start(bf16[8,256,128]{2,1,0:T(8,128)(2,1)} %attn.2), calls=%async_computation.3 | async-start | bytes 1048576 | tf_op jit(solution)/shard_map/all_to_all | solution.py:276
  128.5 2.3 %merge.1 = (bf16[112,128]{1,0:T(8,128)(2,1)}, bf16[112,128]{1,0:T(8,128)(2,1)}, bf16[112,128]{1,0:T(8,128)(2,1)}) custom-call(bf16[8,384,128]{2,1,0:T(8,128)(2,1)} %copy-done.2), custom_call_target="tpu_custom_call" | custom-call | flops 2200000000 | bytes 1048576 | tf_op jit(solution)/shard_map/merge/pallas_call | solution.py:248
  132.3 5.8 %reduce-scatter.4.cloned.1.call-done = bf16[48,480]{1,0:T(8,128)(2,1)} async-done(((bf16[384,480]{1,0:T(8,128)(2,1)}), bf16[48,480]{1,0:T(8,128)(2,1)}) %reduce-scatter.4.cloned.1.call-update) | async-done | bytes 46096 | tf_op jit(solution)/shard_map/reduce_scatter | solution.py:362
  139.8 6.6 %all-to-all-done.3.ref = bf16[8,256,128]{2,1,0:T(8,128)(2,1)S(1)} async-done(((bf16[8,256,128]{2,1,0:T(8,128)(2,1)}), bf16[8,256,128]{2,1,0:T(8,128)(2,1)S(1)}, u32[]{:S(2)}, u32[]{:S(2)}) %all-to-all-start.3) | async-done | bytes 524320 | tf_op jit(solution)/shard_map/all_to_all | solution.py:276
  147.2 2.2 %finish.1 = bf16[112,640]{1,0:T(8,128)(2,1)} custom-call(bf16[8,256,128]{2,1,0:T(8,128)(2,1)} %copy-done.3, bf16[112,128]{1,0:T(8,128)(2,1)} %copy-done.8, bf16[112,128]{1,0:T(8,128)(2,1)} %copy-done.9, bf16[112,128]{1,0:T(8,128)(2,1)} %copy-done.10), custom_call_target="tpu_custom_call" | custom-call | flops 2200000000 | bytes 1048576 | tf_op jit(solution)/shard_map/finish/pallas_call | solution.py:267
  (70 shorter events, 16.5 us)
Async XLA Ops:
  7.2 32.2 %all-gather.4.cloned.1.call-start = ((), (), s32[]{:S(2)}) async-start(), calls=%async_computation.6 | async-start | bytes 1327104 | tf_op jit(solution)/shard_map/all_gather | solution.py:325
  10.8 11.5 %all-to-all-start = ((bf16[4,112,128]{2,1,0:T(8,128)(2,1)}), bf16[4,112,128]{2,1,0:T(8,128)(2,1)S(1)}, u32[]{:S(2)}, u32[]{:S(2)}) async-start(bf16[4,112,128]{2,1,0:T(8,128)(2,1)} %get-tuple-element.162), calls=%async_computation | async-start | bytes 229376 | tf_op jit(solution)/shard_map/all_to_all | solution.py:276
  19.9 45.0 %collective-permute-start = (bf16[1360,256]{1,0:T(8,128)(2,1)}, bf16[1360,256]{1,0:T(8,128)(2,1)}, u32[]{:S(2)}, u32[]{:S(2)}) collective-permute-start(bf16[1360,256]{1,0:T(8,128)(2,1)} %get-tuple-element.169), channel_id=1, source_target_pairs={{0,64},{8,72},{16,80},{24,88},{32,96},{40,104},{48,112},{56,120},{... | collective-permute-start | bytes 2088968 | tf_op jit(solution)/shard_map/ppermute | solution.py:291
  19.9 45.0 %collective-permute-start.1 = (bf16[1360,256]{1,0:T(8,128)(2,1)}, bf16[1360,256]{1,0:T(8,128)(2,1)}, u32[]{:S(2)}, u32[]{:S(2)}) collective-permute-start(bf16[1360,256]{1,0:T(8,128)(2,1)} %get-tuple-element.170), channel_id=1, source_target_pairs={{0,128},{8,136},{16,144},{24,152},{32,160},{40,168},{48,176},{56,1... | collective-permute-start | bytes 2088968 | tf_op jit(solution)/shard_map/ppermute | solution.py:291
  22.3 42.7 %collective-permute-start.2 = (bf16[1360,256]{1,0:T(8,128)(2,1)}, bf16[1360,256]{1,0:T(8,128)(2,1)}, u32[]{:S(2)}, u32[]{:S(2)}) collective-permute-start(bf16[1360,256]{1,0:T(8,128)(2,1)} %get-tuple-element.171), channel_id=1, source_target_pairs={{0,192},{8,200},{16,208},{24,216},{32,224},{40,232},{48,240},{56,2... | collective-permute-start | bytes 2088968 | tf_op jit(solution)/shard_map/ppermute | solution.py:291
  22.4 17.8 %copy-start = (bf16[48,1440]{1,0:T(8,128)(2,1)S(1)}, bf16[48,1440]{1,0:T(8,128)(2,1)}, u32[]{:S(2)}) copy-start(bf16[48,1440]{1,0:T(8,128)(2,1)} %reshape.34) | copy-start | bytes 414724
  22.4 17.8 %copy-start.6 = (f32[48]{0:T(128)S(1)}, f32[48]{0:T(128)}, u32[]{:S(2)}) copy-start(f32[48]{0:T(128)} %param.19) | copy-start | bytes 580
  23.4 41.6 %all-to-all-start.1 = ((bf16[8,336,128]{2,1,0:T(8,128)(2,1)}), bf16[8,336,128]{2,1,0:T(8,128)(2,1)}, u32[]{:S(2)}, u32[]{:S(2)}) async-start(bf16[8,336,128]{2,1,0:T(8,128)(2,1)} %broadcast_in_dim.25), calls=%async_computation.1 | async-start | bytes 1376256 | tf_op jit(solution)/shard_map/all_to_all | solution.py:276
  31.6 71.2 %all-gather.6.cloned.1.call-start = ((), (), s32[]{:S(2)}) async-start(), calls=%async_computation.7 | async-start | bytes 3481600 | tf_op jit(solution)/shard_map/all_gather | solution.py:302
  40.2 11.4 %copy-start.5 = (bf16[112,128]{1,0:T(8,128)(2,1)S(1)}, bf16[112,128]{1,0:T(8,128)(2,1)}, u32[]{:S(2)}) copy-start(bf16[112,128]{1,0:T(8,128)(2,1)} %get-tuple-element.168) | copy-start | bytes 86020
  44.2 10.2 %collective-permute-start.3 = (bf16[48,3,1,160]{0,3,2,1:T(8,128)(2,1)S(1)}, bf16[48,3,1,160]{0,3,2,1:T(8,128)(2,1)S(1)}, u32[]{:S(2)}, u32[]{:S(2)}) collective-permute-start(bf16[48,3,1,160]{0,3,2,1:T(8,128)(2,1)S(1)} %get-tuple-element.278), channel_id=1, source_target_pairs={{0,8},{8,16},{16,24},{24,32},{32,40},{40,48},{48,56},{56,64},{64,7... | collective-permute-start | bytes 138248 | tf_op jit(solution)/shard_map/ppermute | solution.py:340
  47.4 7.0 %collective-permute-start.4 = (bf16[48,3,1,160]{0,3,2,1:T(8,128)(2,1)S(1)}, bf16[48,3,1,160]{0,3,2,1:T(8,128)(2,1)S(1)}, u32[]{:S(2)}, u32[]{:S(2)}) collective-permute-start(bf16[48,3,1,160]{0,3,2,1:T(8,128)(2,1)S(1)} %get-tuple-element.277), channel_id=1, source_target_pairs={{8,0},{16,8},{24,16},{32,24},{40,32},{48,40},{56,48},{64,56},{72,6... | collective-permute-start | bytes 138248 | tf_op jit(solution)/shard_map/ppermute | solution.py:341
  64.9 7.4 %copy-start.1 = (bf16[384,480]{0,1:T(8,128)(2,1)S(1)}, bf16[384,480]{0,1:T(8,128)(2,1)}, u32[]{:S(2)}) copy-start(bf16[384,480]{0,1:T(8,128)(2,1)} %get-tuple-element.184) | copy-start | bytes 1105924
  65.9 24.4 %all-to-all-start.2 = ((bf16[8,224,128]{2,1,0:T(8,128)(2,1)}), bf16[8,224,128]{2,1,0:T(8,128)(2,1)S(1)}, u32[]{:S(2)}, u32[]{:S(2)}) async-start(bf16[8,224,128]{2,1,0:T(8,128)(2,1)} %broadcast_in_dim.26), calls=%async_computation.2 | async-start | bytes 917504 | tf_op jit(solution)/shard_map/all_to_all | solution.py:276
  72.1 66.0 %reduce-scatter.4.cloned.1.call-start = ((), (), s32[]{:S(2)}) async-start(), calls=%async_computation.8 | async-start | bytes 442368 | tf_op jit(solution)/shard_map/reduce_scatter | solution.py:362
  90.3 12.4 %copy-start.4 = (bf16[8,224,128]{2,1,0:T(8,128)(2,1)}, bf16[8,224,128]{2,1,0:T(8,128)(2,1)S(1)}, u32[]{:S(2)}) copy-start(bf16[8,224,128]{2,1,0:T(8,128)(2,1)S(1)} %all-to-all-done.2.q_ref) | copy-start | bytes 1376260
  90.3 29.4 %all-to-all-start.4 = ((bf16[8,384,128]{2,1,0:T(8,128)(2,1)}), bf16[8,384,128]{2,1,0:T(8,128)(2,1)S(1)}, u32[]{:S(2)}, u32[]{:S(2)}) async-start(bf16[8,384,128]{2,1,0:T(8,128)(2,1)} %attn.3), calls=%async_computation.4 | async-start | bytes 1572864 | tf_op jit(solution)/shard_map/all_to_all | solution.py:276
  119.7 8.8 %copy-start.2 = (bf16[8,384,128]{2,1,0:T(8,128)(2,1)}, bf16[8,384,128]{2,1,0:T(8,128)(2,1)S(1)}, u32[]{:S(2)}) copy-start(bf16[8,384,128]{2,1,0:T(8,128)(2,1)S(1)} %all-to-all-done.4.ref) | copy-start | bytes 2359300
  119.7 26.7 %all-to-all-start.3 = ((bf16[8,256,128]{2,1,0:T(8,128)(2,1)}), bf16[8,256,128]{2,1,0:T(8,128)(2,1)S(1)}, u32[]{:S(2)}, u32[]{:S(2)}) async-start(bf16[8,256,128]{2,1,0:T(8,128)(2,1)} %attn.2), calls=%async_computation.3 | async-start | bytes 1048576 | tf_op jit(solution)/shard_map/all_to_all | solution.py:276
  128.5 9.6 %copy-start.7 = (f32[48]{0:T(128)S(1)}, f32[48]{0:T(128)}, u32[]{:S(2)}) copy-start(f32[48]{0:T(128)} %param.21) | copy-start | bytes 580
  130.8 8.9 %collective-permute-start.5 = (bf16[112,128]{1,0:T(8,128)(2,1)}, bf16[112,128]{1,0:T(8,128)(2,1)S(1)}, u32[]{:S(2)}, u32[]{:S(2)}) collective-permute-start(bf16[112,128]{1,0:T(8,128)(2,1)} %get-tuple-element.181), channel_id=1, source_target_pairs={{0,64},{8,72},{16,80},{24,88},{32,96},{40,104},{48,112},{56,120},{... | collective-permute-start | bytes 86024 | tf_op jit(solution)/shard_map/ppermute | solution.py:307
  130.8 8.9 %collective-permute-start.6 = (bf16[112,128]{1,0:T(8,128)(2,1)}, bf16[112,128]{1,0:T(8,128)(2,1)S(1)}, u32[]{:S(2)}, u32[]{:S(2)}) collective-permute-start(bf16[112,128]{1,0:T(8,128)(2,1)} %get-tuple-element.182), channel_id=1, source_target_pairs={{0,128},{8,136},{16,144},{24,152},{32,160},{40,168},{48,176},{56,1... | collective-permute-start | bytes 86024 | tf_op jit(solution)/shard_map/ppermute | solution.py:307
  130.8 8.9 %collective-permute-start.7 = (bf16[112,128]{1,0:T(8,128)(2,1)}, bf16[112,128]{1,0:T(8,128)(2,1)S(1)}, u32[]{:S(2)}, u32[]{:S(2)}) collective-permute-start(bf16[112,128]{1,0:T(8,128)(2,1)} %get-tuple-element.183), channel_id=1, source_target_pairs={{0,192},{8,200},{16,208},{24,216},{32,224},{40,232},{48,240},{56,2... | collective-permute-start | bytes 86024 | tf_op jit(solution)/shard_map/ppermute | solution.py:307
  139.7 6.7 %copy-start.8 = (bf16[112,128]{1,0:T(8,128)(2,1)}, bf16[112,128]{1,0:T(8,128)(2,1)S(1)}, u32[]{:S(2)}) copy-start(bf16[112,128]{1,0:T(8,128)(2,1)S(1)} %collective-permute-done.5.refs_0_) | copy-start | bytes 86020
  (3 other events, 14.1 us)
Sparse Core Ops, SparseCore 0:
  9.8 29.5 all-gather.3
  65.1 37.6 all-gather.5
  105.3 32.7 reduce-scatter.3
where the time goes:
time: 157 us; the launch traced here: 156 us
  starting transfers between devices  46.7 us (30%)
  Pallas kernels  44.2 us (28%)
  waiting for transfers between devices  27.8 us (18%)
  local copies, waits for them, and re-layouts  16.9 us (11%)
  between operations  14.6 us (9%)
  matrix products  2.87 us (2%)
  other arithmetic  2.86 us (2%)
    all_to_all x5, starting transfers between devices, exchange(): return lax.all_to_all(value, axis, 0, 0, axis_index_groups=groups)  35.1 us
    pallas_call x2, Pallas kernels, attn(): pl.pallas_call(functools.partial(attn_kernel, slots, part, rows, c2), out...  33.8 us
    all_gather x1, waiting for transfers between devices, conv_terms(): whole = lax.all_gather(flat, 'head', axis=0, tiled=True)  7.77 us
    all_to_all x5, waiting for transfers between devices, exchange(): return lax.all_to_all(value, axis, 0, 0, axis_index_groups=groups)  6.77 us
    reduce_scatter x1, waiting for transfers between devices, conv_sum(): total = lax.psum_scatter(terms, 'head', scatter_dimension=0, tiled=True)  5.8 us
    all_gather x1, waiting for transfers between devices, attention_part(): lax.all_gather(last_cache, 'hist', axis=0, axis_index_groups=ALONG_X)  4.69 us
    pallas_call x1, Pallas kernels, pack_cache(): pl.pallas_call(pack_cache_kernel, in_specs=[smem, vmem, vmem], out_shape=...  4.29 us
    ppermute x1, starting transfers between devices, conv_terms(): high = lax.ppermute(act[:, :, :1], 'hist', backward)  4.21 us
  transfers between devices with their start and end apart: 16, of which 6 were waited for; matrix products, arithmetic and copies ran while one was open for 13% of the time, Pallas kernels for 27%

commit v1 on v0

v1 whole, which is shorter than its diff:
```python
import functools
import math

import jax
import jax.numpy as jnp
from jax import lax
from jax.experimental import pallas as pl
from jax.experimental.pallas import tpu as pltpu
from jax.sharding import PartitionSpec as P

HEAD_DIM = 128
CHANNELS = 384
NX = 4
NZ = 8
NY = 4

NEG = -1e30
LOG2E = math.log2(math.e)
norm_eps = 1e-06
VMEM = 56 << 20
SIZES = (640, 1024)

HIST = ("x", "z")

vmem = pl.BlockSpec(memory_space=pltpu.VMEM)
smem = pl.BlockSpec(memory_space=pltpu.SMEM)


def head_shift(dy, flip):
    return [
        (y * 2 + c, ((y + dy) % NY) * 2 + (c ^ flip)) for y in range(NY) for c in range(2)
    ]


def head_swap(bit):
    return [(i, i ^ bit) for i in range(2 * NY)]


def dot(a, b, dims):
    return lax.dot_general(a, b, (dims, ((), ())), preferred_element_type=jnp.float32)


def cost(micros, nbytes):
    return pl.CostEstimate(
        flops=int(micros * 1.1e9), bytes_accessed=nbytes, transcendentals=0
    )


def pack_queries_kernel(q_ref, out, last):
    for i in range(NX):
        out[i] = q_ref[:, i * 128 : (i + 1) * 128]
    last[...] = q_ref[:, NX * 128 :]


def pack_queries(queries):
    rows = queries.shape[0]
    return pl.pallas_call(
        pack_queries_kernel,
        out_shape=[
            jax.ShapeDtypeStruct((NX, rows, 128), jnp.bfloat16),
            jax.ShapeDtypeStruct((rows, 128), jnp.bfloat16),
        ],
        cost_estimate=cost(1, 1 << 18),
        name="pack_q",
    )(queries)


def columns(head):
    return pl.ds(pl.multiple_of(head * 128, 128), 128)


def pack_cache_kernel(len_ref, k_ref, v_ref, *outs):
    x = lax.axis_index("x")
    rows = k_ref.shape[0]
    length = len_ref[0]
    row = lax.broadcasted_iota(jnp.int32, (16, 256), 0)
    tail = jnp.where(row == 0, length // 64, jnp.where(row == 1, lax.rem(length, 64), 0))
    tail = tail.astype(jnp.float32).astype(jnp.bfloat16)
    for d, out in enumerate(outs):
        cols = columns(lax.rem(x + d, NX) if d < NX else NX)
        out[:rows, :128] = k_ref[:, cols]
        out[:rows, 128:] = v_ref[:, cols]
        out[rows:, :] = tail


def pack_cache(lengths, keys, values):
    shape = jax.ShapeDtypeStruct((keys.shape[0] + 16, 256), jnp.bfloat16)
    return pl.pallas_call(
        pack_cache_kernel,
        in_specs=[smem, vmem, vmem],
        out_shape=[shape] * (NX + 1),
        compiler_params=pltpu.CompilerParams(vmem_limit_bytes=VMEM),
        cost_estimate=cost(3, 7 << 20),
        name="pack_kv",
    )(lengths, keys, values)


def unit(q_of, n, group, k_of, v_of, limit, rows, acc_ref, l_ref, m_ref, c2):
    def step(low, count):
        row = lax.broadcasted_iota(jnp.int32, (count - low, 128), 0) + low
        seen = row < limit
        first = jnp.broadcast_to(k_of(0, 16).astype(jnp.float32)[:1, :], (count - low, 128))
        k = jnp.where(seen, k_of(low, count).astype(jnp.float32), first).astype(jnp.bfloat16)
        v = jnp.where(seen, v_of(low, count).astype(jnp.float32), 0.0).astype(jnp.bfloat16)
        one = jnp.where(seen, 1.0, 0.0).astype(jnp.bfloat16)
        v = jnp.concatenate([v, one], axis=1)
        if low:
            k = jnp.concatenate([k_of(0, low), k], axis=0)
            ahead = [v_of(0, low), jnp.ones((low, 128), jnp.bfloat16)]
            v = jnp.concatenate([jnp.concatenate(ahead, axis=1), v], axis=0)

        s = dot(q_of(0), k, ((1,), (1,)))
        for g in range(n):
            later = dot(q_of(g + 1), k, ((1,), (1,))) if g + 1 < n else None
            here = slice(g * group, (g + 1) * group)
            old = m_ref[here, :]
            new = jnp.maximum(old, jnp.max(s, axis=1, keepdims=True) * c2)
            p = jnp.exp2(s * c2 - new[:, :1]).astype(jnp.bfloat16)
            r = dot(p, v, ((1,), (0,)))
            a = jnp.exp2(old - new)
            acc_ref[here, :] = acc_ref[here, :] * a + r[:, :128]
            l_ref[here, :] = l_ref[here, :] * a + r[:, 128:]
            m_ref[here, :] = new
            s = later

    low = 0
    for size in SIZES + (rows,):
        pl.when((limit > low) & (limit <= size))(functools.partial(step, low, size))
        low = size


def three_parts(value):
    high = value.astype(jnp.bfloat16).astype(jnp.float32)
    rest = value - high
    mid = rest.astype(jnp.bfloat16).astype(jnp.float32)
    return [high, mid, rest - mid]


def attn_kernel(slots, part, rows, c2, bounds_ref, q_ref, *refs):
    own = slots == 2
    count = 2 * NX if own else NX
    kv_refs, refs = refs[:count], refs[count:]
    out, q_buf, kv, tails, lens, acc_ref, l_ref, m_ref, q_sem, kv_sems, tail_sems = refs
    first = (NX - 1) * part if own else 0
    small = []
    for u, ref in enumerate(kv_refs):
        there = tails.at[u]
        small.append(pltpu.make_async_copy(ref.at[pl.ds(rows, 16), :], there, tail_sems.at[u]))
    for c in small:
        c.start()
    q_copy = pltpu.make_async_copy(q_ref.at[:, pl.ds(first, slots * part), :], q_buf, q_sem)
    q_copy.start()
    for u, ref in enumerate(kv_refs):
        pltpu.make_async_copy(ref, kv.at[u], kv_sems.at[u]).start()
    acc_ref[...] = jnp.zeros_like(acc_ref)
    l_ref[...] = jnp.zeros_like(l_ref)
    m_ref[...] = jnp.full_like(m_ref, NEG)
    x, z = lax.axis_index("x"), lax.axis_index("z")
    many = NZ // 2

    def kv_copy(u):
        return pltpu.make_async_copy(kv_refs[0], kv.at[u], kv_sems.at[u])

    row = lax.broadcasted_iota(jnp.int32, (16, 128), 0)
    for u, c in enumerate(small):
        c.wait()
        tail = tails[u, :, :128].astype(jnp.float32)
        high = jnp.max(jnp.where(row == 0, tail, 0.0))
        low = jnp.max(jnp.where(row == 1, tail, 0.0))
        lens[u] = (high * 64.0 + low).astype(jnp.int32)
    q_copy.wait()

    def body(step, carry):
        if own:
            u, slot, frame = step, step // NX, x
            kv_copy(u).wait()
        else:
            u, slot = step // slots, lax.rem(step, slots)
            frame = lax.rem(x + 1 + slot, NX)
            pl.when(slot == 0)(lambda: kv_copy(u).wait())
        block = lax.rem(x + NX - lax.rem(u, NX), NX) * NZ + z
        at = pl.ds(pl.multiple_of(slot * part, 16), part)
        unit(
            lambda g: q_buf[g * many : (g + 1) * many, at, :].reshape(many * part, 128),
            2,
            many * part,
            lambda a, b: kv[u, a:b, :128],
            lambda a, b: kv[u, a:b, 128:],
            jnp.minimum(lens[u], bounds_ref[frame] - block * rows),
            rows,
            acc_ref.at[slot],
            l_ref.at[slot],
            m_ref.at[slot],
            c2,
        )
        return carry

    lax.fori_loop(0, slots * NX, body, 0)
    lane = lax.broadcasted_iota(jnp.int32, (part, 128), 1)
    fill = jnp.zeros((128 - part, 128), jnp.float32)
    under = slots * part
    empty = jnp.zeros((16 - 5 * slots, 128), jnp.float32)
    for g in range(NZ):
        here = slice(g * part, (g + 1) * part)
        table = jnp.zeros((part, 128), jnp.float32)
        for slot in range(slots):
            out[g, slot * part : (slot + 1) * part, :] = acc_ref[slot, here, :].astype(jnp.bfloat16)
            table = jnp.where(lane == slot, m_ref[slot, here, :], table)
            table = jnp.where(lane == slots + slot, l_ref[slot, here, :], table)
        flat = jnp.concatenate([table, fill], axis=0).T
        pieces = three_parts(flat[:slots, :]) + three_parts(flat[slots : 2 * slots, :])[:2]
        flat = jnp.concatenate(pieces + [empty], axis=0)
        out[g, under : under + 16, :] = flat.astype(jnp.bfloat16)


def attn(bounds, queries, kvs, part, c2):
    rows = kvs[0].shape[0] - 16
    slots = NX - 1 if len(kvs) == NX else 2
    anys = pl.BlockSpec(memory_space=pl.ANY)
    return pl.pallas_call(
        functools.partial(attn_kernel, slots, part, rows, c2),
        out_shape=jax.ShapeDtypeStruct((NZ, slots * part + 16, 128), jnp.bfloat16),
        in_specs=[smem, anys] + [anys] * len(kvs),
        out_specs=vmem,
        scratch_shapes=[
            pltpu.VMEM((NZ, slots * part, 128), jnp.bfloat16),
            pltpu.VMEM((len(kvs), rows + 16, 256), jnp.bfloat16),
            pltpu.VMEM((len(kvs), 16, 256), jnp.bfloat16),
            pltpu.SMEM((len(kvs),), jnp.int32),
        ]
        + [pltpu.VMEM((slots, NZ * part, 128), jnp.float32)] * 3
        + [pltpu.SemaphoreType.DMA] + [pltpu.SemaphoreType.DMA((len(kvs),))] * 2,
        compiler_params=pltpu.CompilerParams(vmem_limit_bytes=VMEM),
        cost_estimate=cost(8 * slots, 1 << 20),
        name="attn",
    )(bounds, queries, *kvs)


def merge_z(ref, part, slots, slot):
    under = slice(slots * part, slots * part + 16)
    tops, totals = [], []
    for s in range(NZ):
        rows16 = ref[s, under, :].astype(jnp.float32)
        pieces = [rows16[k * slots + slot : k * slots + slot + 1, :] for k in range(5)]
        tops.append(pieces[0] + pieces[1] + pieces[2])
        totals.append(pieces[3] + pieces[4])
    top = functools.reduce(jnp.maximum, tops)
    raw = [jnp.exp2(t - top) for t in tops]
    total = functools.reduce(jnp.add, [r * t for r, t in zip(raw, totals)])
    total = jnp.maximum(total, 1.0)
    fill = jnp.zeros((128 - NZ, 128), jnp.float32)
    table = jnp.concatenate([r / total for r in raw] + [fill], axis=0).T
    out = jnp.zeros((part, 128), jnp.float32)
    for s in range(NZ):
        data = ref[s, slot * part : (slot + 1) * part, :].astype(jnp.float32)
        out += table[:part, s : s + 1] * data
    return out.astype(jnp.bfloat16)


def merge_kernel(part, ref, *outs):
    for slot, out in enumerate(outs):
        out[...] = merge_z(ref, part, len(outs), slot)


def merge(payload, part):
    return pl.pallas_call(
        functools.partial(merge_kernel, part),
        out_shape=[jax.ShapeDtypeStruct((part, 128), jnp.bfloat16)] * (NX - 1),
        cost_estimate=cost(2, 1 << 20),
        name="merge",
    )(payload)


def finish_kernel(part, ref, *refs):
    others, out = refs[: NX - 1], refs[NX - 1]
    x = lax.axis_index("x")
    out[:, pl.ds(pl.multiple_of(x * 128, 128), 128)] = merge_z(ref, part, 2, 0)
    out[:, NX * 128 :] = merge_z(ref, part, 2, 1)
    for k, r in enumerate(others):
        head = lax.rem(x + NX - 1 - k, NX)
        out[:, pl.ds(pl.multiple_of(head * 128, 128), 128)] = r[...]


def finish(payload, others, part):
    return pl.pallas_call(
        functools.partial(finish_kernel, part),
        out_shape=jax.ShapeDtypeStruct((part, (NX + 1) * 128), jnp.bfloat16),
        cost_estimate=cost(2, 1 << 20),
        name="finish",
    )(payload, *others)


def exchange(value, axis):
    return lax.all_to_all(value, axis, 0, 0)


def along_x(value, dx):
    return lax.ppermute(value, "x", [(x, (x + dx) % NX) for x in range(NX)])


def attention_part(queries, keys, values, length, bounds, conv):
    part = queries.shape[0]
    c2 = HEAD_DIM ** (-0.5) * LOG2E
    x = lax.axis_index("x")
    packed, last = pack_queries(queries)
    mine = exchange(packed, "x")
    keys, values, _ = lax.optimization_barrier((keys, values, packed))
    cache = pack_cache(length, keys, values)
    kvs = [cache[0]] + [along_x(cache[d], d) for d in range(1, NX)]
    order = lax.dynamic_slice_in_dim(jnp.concatenate([mine, mine]), x + 1, NX, 0)
    order = jnp.concatenate([order.reshape(NX * part, 128), last], axis=0)
    order, _ = lax.optimization_barrier((order, cache[0]))
    everyone = exchange(jnp.broadcast_to(order[None], (NZ,) + order.shape), "z")
    last, kvs, terms, everyone = lax.optimization_barrier(
        (cache[NX], kvs, conv(cache[0]), everyone)
    )
    lasts = [last] + [along_x(last, d) for d in range(1, NX)]

    landed = exchange(attn(bounds, everyone, kvs, part, c2), "z")
    landed_own = exchange(attn(bounds, everyone, kvs + lasts, part, c2), "z")
    others = [along_x(r, i + 1) for i, r in enumerate(merge(landed, part))]
    return finish(landed_own, others, part), terms


def once(fun, *args):
    shapes = jax.eval_shape(fun, *args)
    turns = 1 + lax.axis_index("x") // NX

    def body(_, carry):
        return lax.optimization_barrier((carry[0], fun(*carry[0])))

    return lax.fori_loop(0, turns, body, (args, jnp.zeros(shapes.shape, shapes.dtype)))[1]


def conv_terms(low, latent, high, norm_gain, conv_weight):
    channels, _, rows, width = latent.shape
    wide = jnp.concatenate([low, latent, high], axis=2)
    squares = jnp.sum(jnp.square(wide.astype(jnp.float32)), axis=0)
    for bit in (1, 2, 4):
        squares = squares + lax.ppermute(squares, "head", head_swap(bit))
    scaled = (
        wide.astype(jnp.float32)
        * lax.rsqrt(squares / CHANNELS + norm_eps)[None]
        * norm_gain[:, None, None, None]
    )
    act = jax.nn.silu(scaled).astype(jnp.bfloat16)
    padded = jnp.pad(act, ((0, 0), (0, 0), (0, 0), (1, 1)))
    windows = [
        padded[:, a, b : b + rows, e : e + width]
        for a in range(3)
        for b in range(3)
        for e in range(3)
    ]
    patches = jnp.concatenate(windows, axis=0)
    weight = conv_weight.reshape(27 * channels, conv_weight.shape[4])
    terms = jnp.einsum("kyx,ko->oyx", patches, weight, preferred_element_type=jnp.float32)
    return terms.astype(jnp.bfloat16).reshape(-1, rows * width)


def neighbour_rows(latent):
    count = lax.axis_size(HIST)
    forward = [(i, i + 1) for i in range(count - 1)]
    backward = [(b, a) for a, b in forward]
    low = lax.ppermute(latent[:, :, -1:], HIST, forward)
    high = lax.ppermute(latent[:, :, :1], HIST, backward)
    return low, high


def conv_sum(terms, conv_bias, shape):
    terms = terms.reshape(NY, 2, shape[0], -1)
    core = lax.rem(lax.axis_index("head"), 2)
    y = lax.axis_index("head") // 2
    kept = lax.dynamic_index_in_dim(terms, core, 1, keepdims=False)
    given = lax.dynamic_index_in_dim(terms, 1 - core, 1, keepdims=False)
    given = lax.ppermute(given, "head", head_swap(1))
    both = kept.astype(jnp.float32) + given.astype(jnp.float32)
    total = lax.dynamic_index_in_dim(both, y, 0, keepdims=False)
    sent = both.astype(jnp.bfloat16)
    for d in range(1, NY):
        piece = lax.dynamic_index_in_dim(sent, lax.rem(y + d, NY), 0, keepdims=False)
        total = total + lax.ppermute(piece, "head", head_shift(d, 0)).astype(jnp.float32)
    out = (total + conv_bias[:, None]).astype(jnp.bfloat16)
    return out.reshape(shape)


def on_device(
    queries,
    cache_keys,
    cache_values,
    hist_lengths,
    frame_bounds,
    latent,
    norm_gain,
    conv_weight,
    conv_bias,
):
    low, high = neighbour_rows(latent)
    attention, terms = attention_part(
        queries,
        cache_keys,
        cache_values,
        hist_lengths,
        frame_bounds,
        lambda after: once(
            conv_terms,
            low,
            lax.optimization_barrier((latent, after))[0],
            high,
            norm_gain,
            conv_weight,
        ),
    )
    shape = (latent.shape[0], latent.shape[2], latent.shape[3])
    return (attention, conv_sum(terms, conv_bias, shape))


def solution(mesh):
    split = jax.sharding.Mesh(
        mesh.devices.reshape(NX, NZ, mesh.shape["head"]), ("x", "z", "head")
    )
    hist = ("x", "z")
    placed = (
        P(hist, "head"),
        P(hist, "head"),
        P(hist, "head"),
        P(hist),
        P(),
        P("head", None, hist, None),
        P("head"),
        P(None, None, None, "head", None),
        P("head"),
    )
    return jax.shard_map(
        on_device,
        mesh=split,
        in_specs=placed,
        out_specs=(P(hist, "head"), P("head", hist, None)),
        check_vma=False,
    )
```

time: 157 us -> 138 us (0.88)
  the two profiles are of different devices: /device:TPU:7 before, /device:TPU:8 now
where the time goes in v1:
time: 138 us; the launch traced here: 136 us
  starting transfers between devices  50.6 us (37%)
  Pallas kernels  42.3 us (31%)
  waiting for transfers between devices  25.9 us (19%)
  local copies, waits for them, and re-layouts  11.2 us (8%)
  matrix products  2.84 us (2%)
  between operations  1.59 us (1%)
    pallas_call x2, Pallas kernels, attn(): pl.pallas_call(functools.partial(attn_kernel, slots, part, rows, c2), out...  31.9 us
    all_to_all x4, starting transfers between devices, exchange(): return lax.all_to_all(value, axis, 0, 0)  22 us
    ppermute x9, starting transfers between devices, along_x(): return lax.ppermute(value, 'x', [(x, (x + dx) % NX) for x in range(NX)])  15.6 us
    all_to_all x4, waiting for transfers between devices, exchange(): return lax.all_to_all(value, axis, 0, 0)  11.1 us
    ppermute x3, waiting for transfers between devices, conv_terms(): squares = squares + lax.ppermute(squares, 'head', head_swap(bit))  7.59 us
    ppermute x9, waiting for transfers between devices, along_x(): return lax.ppermute(value, 'x', [(x, (x + dx) % NX) for x in range(NX)])  7.15 us
    ppermute x3, starting transfers between devices, conv_sum(): lax.ppermute(piece, 'head', head_shift(d, 0)).astype(jnp.float32)  5.01 us
    pallas_call x1, Pallas kernels, pack_cache(): pl.pallas_call(pack_cache_kernel, in_specs=[smem, vmem, vmem], out_shape=...  4.34 us
  transfers between devices with their start and end apart: 22, of which 9 were waited for; matrix products, arithmetic and copies ran while one was open for 10% of the time, Pallas kernels for 28%

profile of v1, /device:TPU:8, one launch (start us, length us, event | category | flops | bytes accessed | tf_op | source)
XLA Modules:
  0.0 135.8 jit_solution(18008660661826098251)
XLA Ops:
  2.2 4.3 %all-to-all-start = ((bf16[4,112,128]{2,1,0:T(8,128)(2,1)}), bf16[4,112,128]{2,1,0:T(8,128)(2,1)S(1)}, u32[]{:S(2)}, u32[]{:S(2)}) async-start(bf16[4,112,128]{2,1,0:T(8,128)(2,1)} %get-tuple-element.141), calls=%async_computation | async-start | bytes 229376 | tf_op jit(solution)/shard_map/all_to_all | solution.py:294
  7.2 4.3 %pack_kv.1 = (bf16[1360,256]{1,0:T(8,128)(2,1)}, bf16[1360,256]{1,0:T(8,128)(2,1)}, bf16[1360,256]{1,0:T(8,128)(2,1)}, bf16[1360,256]{1,0:T(8,128)(2,1)}, bf16[1360,256]{1,0:T(8,128)(2,1)}) custom-call(s32[1]{0:T(128)S(6)} %copy.27.len_ref, bf16[1344,640]{1,0:T(8,128)(2,1)} %k_ref, bf16[1344,640]{1,0:T(8,128)(2,1)} %v_ref), custom_call_target="tpu_custom_call" | custom-call | flops 3300000000 | bytes 7340032 | tf_op jit(solution)/shard_map/pack_kv/pallas_call | solution.py:88
  11.5 2.0 %collective-permute-start.3 = (bf16[1360,256]{1,0:T(8,128)(2,1)}, bf16[1360,256]{1,0:T(8,128)(2,1)}, u32[]{:S(2)}, u32[]{:S(2)}) collective-permute-start(bf16[1360,256]{1,0:T(8,128)(2,1)} %get-tuple-element.146), channel_id=1, source_target_pairs={{0,64},{64,128},{128,192},{192,0},{1,65},{65,129},{129,193},{193,1... | collective-permute-start | bytes 2088968 | tf_op jit(solution)/shard_map/ppermute | solution.py:298
  13.5 2.7 %collective-permute-start.4 = (bf16[1360,256]{1,0:T(8,128)(2,1)}, bf16[1360,256]{1,0:T(8,128)(2,1)}, u32[]{:S(2)}, u32[]{:S(2)}) collective-permute-start(bf16[1360,256]{1,0:T(8,128)(2,1)} %get-tuple-element.147), channel_id=1, source_target_pairs={{0,128},{64,192},{128,0},{192,64},{1,129},{65,193},{129,1},{193,65... | collective-permute-start | bytes 2088968 | tf_op jit(solution)/shard_map/ppermute | solution.py:298
  16.4 3.8 %collective-permute-start.6 = (bf16[48,3,1,160]{0,3,2,1:T(8,128)(2,1)S(1)}, bf16[48,3,1,160]{0,3,2,1:T(8,128)(2,1)S(1)}, u32[]{:S(2)}, u32[]{:S(2)}) collective-permute-start(bf16[48,3,1,160]{0,3,2,1:T(8,128)(2,1)S(1)} %copy.19), channel_id=1, source_target_pairs={{0,8},{8,16},{16,24},{24,32},{32,40},{40,48},{48,56},{56,64},{64,7... | collective-permute-start | bytes 138248 | tf_op jit(solution)/shard_map/ppermute | solution.py:364
  23.2 10.5 %all-to-all-start.1 = ((bf16[8,560,128]{2,1,0:T(8,128)(2,1)}), bf16[8,560,128]{2,1,0:T(8,128)(2,1)}, u32[]{:S(2)}, u32[]{:S(2)}) async-start(bf16[8,560,128]{2,1,0:T(8,128)(2,1)} %broadcast_in_dim.5), calls=%async_computation.1 | async-start | bytes 2293760 | tf_op jit(solution)/shard_map/all_to_all | solution.py:294
  36.0 20.3 %while.22 = (s32[]{:T(128)}, bf16[48,3,1,160]{0,3,2,1:T(8,128)(2,1)S(1)}, bf16[48,3,3,160]{0,3,2,1:T(8,128)(2,1)S(1)}, bf16[48,3,1,160]{0,3,2,1:T(8,128)(2,1)S(1...) while((s32[]{:T(128)}, ...), condition=%wide.region_2.3_spmd, body=%wide.region_0.2_spmd.sunk | while | flops 479679360 | bytes 10202133 | solution.py:332
  38.3 3.4 %collective-permute-done.1 = f32[3,5,160]{2,1,0:T(8,128)S(1)} collective-permute-done((f32[3,5,160]{2,1,0:T(8,128)S(1)}, f32[3,5,160]{2,1,0:T(8,128)S(1)}, u32[]{:S(2)}, u32[]{:S(2)}) %collective-permute-start.1) | collective-permute-done | bytes 9632 | tf_op jit(solution)/shard_map/while/body/ppermute | solution.py:340
  41.7 2.3 %collective-permute-start.2 = (f32[3,5,160]{2,1,0:T(8,128)S(1)}, f32[3,5,160]{2,1,0:T(8,128)S(1)}, u32[]{:S(2)}, u32[]{:S(2)}) collective-permute-start(f32[3,5,160]{2,1,0:T(8,128)S(1)} %add.168), channel_id=1, source_target_pairs={{0,4},{1,5},{2,6},{3,7},{4,0},{5,1},{6,2},{7,3},{8,12},{9,13},{10,... | collective-permute-start | bytes 28808 | tf_op jit(solution)/shard_map/while/body/ppermute | solution.py:340
  44.0 3.0 %collective-permute-done.2 = f32[3,5,160]{2,1,0:T(8,128)S(1)} collective-permute-done((f32[3,5,160]{2,1,0:T(8,128)S(1)}, f32[3,5,160]{2,1,0:T(8,128)S(1)}, u32[]{:S(2)}, u32[]{:S(2)}) %collective-permute-start.2) | collective-permute-done | bytes 9632 | tf_op jit(solution)/shard_map/while/body/ppermute | solution.py:340
  49.7 3.7 %concatenate.21 = bf16[1296,3,160]{0,2,1:T(8,128)(2,1)S(1)} concatenate(bf16[48,3,160]{0,2,1:T(8,128)(2,1)} %get-tuple-element.312, bf16[48,3,160]{0,2,1:T(8,128)(2,1)} %get-tuple-element.313, bf16[48,3,160]{0,2,1:T(8,128)(2,1)} %get-tuple-element.314, bf16[48,3,160]{0,2,1:T(8,128)(2,1)} %get-tuple-element.315, bf16[48,3,160]{0,2,1:T(8,128)(2,1)} %get-tuple-element.316, ...), dimensions={0} | concatenate | bytes 2488320 | tf_op jit(solution)/shard_map/while/body/concatenate | solution.py:354
  53.5 2.8 %convolution_convert_fusion.2 = bf16[3,160,384]{2,1,0:T(8,128)(2,1)} fusion(bf16[1296,3,160]{0,2,1:T(8,128)(2,1)S(1)} %concatenate.21, bf16[1296,384,1]{1,0,2:T(8,128)(2,1)} %bitcast.104), kind=kOutput, calls=%fused_computation.2.clone.1 | convolution fusion | flops 477941760 | bytes 2608128 | tf_op jit(solution)/shard_map/while/body/kyx,ko->oyx/dot_general | solution.py:356
  56.3 6.7 %all-to-all-done.1.q_ref = bf16[8,560,128]{2,1,0:T(8,128)(2,1)} async-done(((bf16[8,560,128]{2,1,0:T(8,128)(2,1)}), bf16[8,560,128]{2,1,0:T(8,128)(2,1)}, u32[]{:S(2)}, u32[]{:S(2)}) %all-to-all-start.1) | async-done | bytes 1146912 | tf_op jit(solution)/shard_map/all_to_all | solution.py:294
  63.3 2.6 %collective-permute-start.9 = (bf16[1360,256]{1,0:T(8,128)(2,1)}, bf16[1360,256]{1,0:T(8,128)(2,1)S(1)}, u32[]{:S(2)}, u32[]{:S(2)}) collective-permute-start(bf16[1360,256]{1,0:T(8,128)(2,1)} %get-tuple-element.158.refs_4_), channel_id=1, source_target_pairs={{0,128},{64,192},{128,0},{192,64},{1,129},{65,193},{129,1},{193,65... | collective-permute-start | bytes 2088968 | tf_op jit(solution)/shard_map/ppermute | solution.py:298
  66.5 21.4 %attn.3 = bf16[8,352,128]{2,1,0:T(8,128)(2,1)} custom-call(s32[4]{0:T(128)} %bounds_ref.3, bf16[8,560,128]{2,1,0:T(8,128)(2,1)} %all-to-all-done.1.q_ref, bf16[1360,256]{1,0:T(8,128)(2,1)} %get-tuple-element.154.refs_0_, bf16[1360,256]{1,0:T(8,128)(2,1)} %collective-permute-done.3.refs_1_, bf16[1360,256]{1,0:T(8,128)(2,1)} %collective-permute-done.4.refs_2_, ...), custom_call_target="tpu_custom_call" | custom-call | flops 26400000000 | bytes 1048576 | tf_op jit(solution)/shard_map/attn/pallas_call | solution.py:220
  87.9 3.7 %all-to-all-start.3 = ((bf16[8,352,128]{2,1,0:T(8,128)(2,1)}), bf16[8,352,128]{2,1,0:T(8,128)(2,1)S(1)}, u32[]{:S(2)}, u32[]{:S(2)}) async-start(bf16[8,352,128]{2,1,0:T(8,128)(2,1)} %attn.3), calls=%async_computation.3 | async-start | bytes 1441792 | tf_op jit(solution)/shard_map/all_to_all | solution.py:294
  92.0 3.2 %collective-permute-done.8.refs_5_ = bf16[1360,256]{1,0:T(8,128)(2,1)S(1)} collective-permute-done((bf16[1360,256]{1,0:T(8,128)(2,1)}, bf16[1360,256]{1,0:T(8,128)(2,1)S(1)}, u32[]{:S(2)}, u32[]{:S(2)}) %collective-permute-start.8) | collective-permute-done | bytes 696352 | tf_op jit(solution)/shard_map/ppermute | solution.py:298
  96.3 10.5 %attn.2 = bf16[8,240,128]{2,1,0:T(8,128)(2,1)} custom-call(s32[4]{0:T(128)} %bounds_ref.3, bf16[8,560,128]{2,1,0:T(8,128)(2,1)} %all-to-all-done.1.q_ref, bf16[1360,256]{1,0:T(8,128)(2,1)} %get-tuple-element.154.refs_0_, bf16[1360,256]{1,0:T(8,128)(2,1)} %collective-permute-done.3.refs_1_, bf16[1360,256]{1,0:T(8,128)(2,1)} %collective-permute-done.4.refs_2_, ...), custom_call_target="tpu_custom_call" | custom-call | flops 17600000000 | bytes 1048576 | tf_op jit(solution)/shard_map/attn/pallas_call | solution.py:220
  106.8 4.5 %all-to-all-done.3.ref = bf16[8,352,128]{2,1,0:T(8,128)(2,1)S(1)} async-done(((bf16[8,352,128]{2,1,0:T(8,128)(2,1)}), bf16[8,352,128]{2,1,0:T(8,128)(2,1)S(1)}, u32[]{:S(2)}, u32[]{:S(2)}) %all-to-all-start.3) | async-done | bytes 720928 | tf_op jit(solution)/shard_map/all_to_all | solution.py:294
  111.3 3.5 %all-to-all-start.2 = ((bf16[8,240,128]{2,1,0:T(8,128)(2,1)}), bf16[8,240,128]{2,1,0:T(8,128)(2,1)S(1)}, u32[]{:S(2)}, u32[]{:S(2)}) async-start(bf16[8,240,128]{2,1,0:T(8,128)(2,1)} %attn.2), calls=%async_computation.2 | async-start | bytes 983040 | tf_op jit(solution)/shard_map/all_to_all | solution.py:294
  115.4 2.6 %collective-permute-start.16 = (bf16[48,480]{1,0:T(8,128)(2,1)S(1)}, bf16[48,480]{1,0:T(8,128)(2,1)S(1)}, u32[]{:S(2)}, u32[]{:S(2)}) collective-permute-start(bf16[48,480]{1,0:T(8,128)(2,1)S(1)} %get-tuple-element.230), channel_id=1, source_target_pairs={{0,4},{1,5},{2,6},{3,7},{4,0},{5,1},{6,2},{7,3},{8,12},{9,13},{10,... | collective-permute-start | bytes 138248 | tf_op jit(solution)/shard_map/ppermute | solution.py:381
  119.9 2.3 %merge.1 = (bf16[112,128]{1,0:T(8,128)(2,1)}, bf16[112,128]{1,0:T(8,128)(2,1)}, bf16[112,128]{1,0:T(8,128)(2,1)}) custom-call(bf16[8,352,128]{2,1,0:T(8,128)(2,1)} %copy-done.1), custom_call_target="tpu_custom_call" | custom-call | flops 2200000000 | bytes 1048576 | tf_op jit(solution)/shard_map/merge/pallas_call | solution.py:266
  122.7 5.5 %collective-permute-start.12 = (bf16[112,128]{1,0:T(8,128)(2,1)}, bf16[112,128]{1,0:T(8,128)(2,1)S(1)}, u32[]{:S(2)}, u32[]{:S(2)}) collective-permute-start(bf16[112,128]{1,0:T(8,128)(2,1)} %get-tuple-element.160), channel_id=1, source_target_pairs={{0,128},{64,192},{128,0},{192,64},{1,129},{65,193},{129,1},{193,65... | collective-permute-start | bytes 86024 | tf_op jit(solution)/shard_map/ppermute | solution.py:298
  133.6 2.2 %finish.1 = bf16[112,640]{1,0:T(8,128)(2,1)} custom-call(bf16[8,240,128]{2,1,0:T(8,128)(2,1)} %copy-done.3, bf16[112,128]{1,0:T(8,128)(2,1)} %copy-done.9, bf16[112,128]{1,0:T(8,128)(2,1)} %copy-done.10, bf16[112,128]{1,0:T(8,128)(2,1)} %copy-done.11), custom_call_target="tpu_custom_call" | custom-call | flops 2200000000 | bytes 1048576 | tf_op jit(solution)/shard_map/finish/pallas_call | solution.py:285
  (76 shorter events, 22.7 us)
Async XLA Ops:
  2.2 19.7 %all-to-all-start = ((bf16[4,112,128]{2,1,0:T(8,128)(2,1)}), bf16[4,112,128]{2,1,0:T(8,128)(2,1)S(1)}, u32[]{:S(2)}, u32[]{:S(2)}) async-start(bf16[4,112,128]{2,1,0:T(8,128)(2,1)} %get-tuple-element.141), calls=%async_computation | async-start | bytes 229376 | tf_op jit(solution)/shard_map/all_to_all | solution.py:294
  11.5 10.5 %copy-start.4 = (bf16[112,128]{1,0:T(8,128)(2,1)S(1)}, bf16[112,128]{1,0:T(8,128)(2,1)}, u32[]{:S(2)}) copy-start(bf16[112,128]{1,0:T(8,128)(2,1)} %get-tuple-element.151) | copy-start | bytes 86020
  11.5 44.8 %collective-permute-start.3 = (bf16[1360,256]{1,0:T(8,128)(2,1)}, bf16[1360,256]{1,0:T(8,128)(2,1)}, u32[]{:S(2)}, u32[]{:S(2)}) collective-permute-start(bf16[1360,256]{1,0:T(8,128)(2,1)} %get-tuple-element.146), channel_id=1, source_target_pairs={{0,64},{64,128},{128,192},{192,0},{1,65},{65,129},{129,193},{193,1... | collective-permute-start | bytes 2088968 | tf_op jit(solution)/shard_map/ppermute | solution.py:298
  13.5 42.8 %collective-permute-start.4 = (bf16[1360,256]{1,0:T(8,128)(2,1)}, bf16[1360,256]{1,0:T(8,128)(2,1)}, u32[]{:S(2)}, u32[]{:S(2)}) collective-permute-start(bf16[1360,256]{1,0:T(8,128)(2,1)} %get-tuple-element.147), channel_id=1, source_target_pairs={{0,128},{64,192},{128,0},{192,64},{1,129},{65,193},{129,1},{193,65... | collective-permute-start | bytes 2088968 | tf_op jit(solution)/shard_map/ppermute | solution.py:298
  16.4 18.8 %collective-permute-start.6 = (bf16[48,3,1,160]{0,3,2,1:T(8,128)(2,1)S(1)}, bf16[48,3,1,160]{0,3,2,1:T(8,128)(2,1)S(1)}, u32[]{:S(2)}, u32[]{:S(2)}) collective-permute-start(bf16[48,3,1,160]{0,3,2,1:T(8,128)(2,1)S(1)} %copy.19), channel_id=1, source_target_pairs={{0,8},{8,16},{16,24},{24,32},{32,40},{40,48},{48,56},{56,64},{64,7... | collective-permute-start | bytes 138248 | tf_op jit(solution)/shard_map/ppermute | solution.py:364
  20.4 14.8 %collective-permute-start.7 = (bf16[48,3,1,160]{0,3,2,1:T(8,128)(2,1)S(1)}, bf16[48,3,1,160]{0,3,2,1:T(8,128)(2,1)S(1)}, u32[]{:S(2)}, u32[]{:S(2)}) collective-permute-start(bf16[48,3,1,160]{0,3,2,1:T(8,128)(2,1)S(1)} %copy.20), channel_id=1, source_target_pairs={{8,0},{16,8},{24,16},{32,24},{40,32},{48,40},{56,48},{64,56},{72,6... | collective-permute-start | bytes 138248 | tf_op jit(solution)/shard_map/ppermute | solution.py:365
  23.2 12.8 %copy-start.5 = (f32[48]{0:T(128)S(1)}, f32[48]{0:T(128)}, u32[]{:S(2)}) copy-start(f32[48]{0:T(128)} %param.17) | copy-start | bytes 580
  23.2 39.8 %all-to-all-start.1 = ((bf16[8,560,128]{2,1,0:T(8,128)(2,1)}), bf16[8,560,128]{2,1,0:T(8,128)(2,1)}, u32[]{:S(2)}, u32[]{:S(2)}) async-start(bf16[8,560,128]{2,1,0:T(8,128)(2,1)} %broadcast_in_dim.5), calls=%async_computation.1 | async-start | bytes 2293760 | tf_op jit(solution)/shard_map/all_to_all | solution.py:294
  33.7 22.6 %collective-permute-start.5 = (bf16[1360,256]{1,0:T(8,128)(2,1)}, bf16[1360,256]{1,0:T(8,128)(2,1)}, u32[]{:S(2)}, u32[]{:S(2)}) collective-permute-start(bf16[1360,256]{1,0:T(8,128)(2,1)} %get-tuple-element.148), channel_id=1, source_target_pairs={{0,192},{64,0},{128,64},{192,128},{1,193},{65,1},{129,65},{193,129... | collective-permute-start | bytes 2088968 | tf_op jit(solution)/shard_map/ppermute | solution.py:298
  36.6 1.3 collective-permute-start
  37.9 3.8 %collective-permute-start.1 = (f32[3,5,160]{2,1,0:T(8,128)S(1)}, f32[3,5,160]{2,1,0:T(8,128)S(1)}, u32[]{:S(2)}, u32[]{:S(2)}) collective-permute-start(f32[3,5,160]{2,1,0:T(8,128)S(1)} %add.167), channel_id=1, source_target_pairs={{0,2},{1,3},{2,0},{3,1},{4,6},{5,7},{6,4},{7,5},{8,10},{9,11},{10,... | collective-permute-start | bytes 28808 | tf_op jit(solution)/shard_map/while/body/ppermute | solution.py:340
  41.7 5.3 %collective-permute-start.2 = (f32[3,5,160]{2,1,0:T(8,128)S(1)}, f32[3,5,160]{2,1,0:T(8,128)S(1)}, u32[]{:S(2)}, u32[]{:S(2)}) collective-permute-start(f32[3,5,160]{2,1,0:T(8,128)S(1)} %add.168), channel_id=1, source_target_pairs={{0,4},{1,5},{2,6},{3,7},{4,0},{5,1},{6,2},{7,3},{8,12},{9,13},{10,... | collective-permute-start | bytes 28808 | tf_op jit(solution)/shard_map/while/body/ppermute | solution.py:340
  63.0 32.2 %collective-permute-start.8 = (bf16[1360,256]{1,0:T(8,128)(2,1)}, bf16[1360,256]{1,0:T(8,128)(2,1)S(1)}, u32[]{:S(2)}, u32[]{:S(2)}) collective-permute-start(bf16[1360,256]{1,0:T(8,128)(2,1)} %get-tuple-element.158.refs_4_), channel_id=1, source_target_pairs={{0,64},{64,128},{128,192},{192,0},{1,65},{65,129},{129,193},{193,1... | collective-permute-start | bytes 2088968 | tf_op jit(solution)/shard_map/ppermute | solution.py:298
  63.3 31.9 %collective-permute-start.9 = (bf16[1360,256]{1,0:T(8,128)(2,1)}, bf16[1360,256]{1,0:T(8,128)(2,1)S(1)}, u32[]{:S(2)}, u32[]{:S(2)}) collective-permute-start(bf16[1360,256]{1,0:T(8,128)(2,1)} %get-tuple-element.158.refs_4_), channel_id=1, source_target_pairs={{0,128},{64,192},{128,0},{192,64},{1,129},{65,193},{129,1},{193,65... | collective-permute-start | bytes 2088968 | tf_op jit(solution)/shard_map/ppermute | solution.py:298
  65.9 30.0 %collective-permute-start.10 = (bf16[1360,256]{1,0:T(8,128)(2,1)}, bf16[1360,256]{1,0:T(8,128)(2,1)}, u32[]{:S(2)}, u32[]{:S(2)}) collective-permute-start(bf16[1360,256]{1,0:T(8,128)(2,1)} %get-tuple-element.158.refs_4_), channel_id=1, source_target_pairs={{0,192},{64,0},{128,64},{192,128},{1,193},{65,1},{129,65},{193,129... | collective-permute-start | bytes 2088968 | tf_op jit(solution)/shard_map/ppermute | solution.py:298
  87.9 23.3 %all-to-all-start.3 = ((bf16[8,352,128]{2,1,0:T(8,128)(2,1)}), bf16[8,352,128]{2,1,0:T(8,128)(2,1)S(1)}, u32[]{:S(2)}, u32[]{:S(2)}) async-start(bf16[8,352,128]{2,1,0:T(8,128)(2,1)} %attn.3), calls=%async_computation.3 | async-start | bytes 1441792 | tf_op jit(solution)/shard_map/all_to_all | solution.py:294
  91.9 22.9 %collective-permute-start.14 = (bf16[4,48,480]{2,1,0:T(8,128)(2,1)S(1)}, bf16[4,48,480]{2,1,0:T(8,128)(2,1)S(1)}, u32[]{:S(2)}, u32[]{:S(2)}) collective-permute-start(bf16[4,48,480]{2,1,0:T(8,128)(2,1)S(1)} %dynamic-slice_bitcast_fusion), channel_id=1, source_target_pairs={{0,1},{1,0},{2,3},{3,2},{4,5},{5,4},{6,7},{7,6},{8,9},{9,8},{10,11... | collective-permute-start | bytes 552968 | tf_op jit(solution)/shard_map/ppermute | solution.py:375
  111.3 21.0 %all-to-all-start.2 = ((bf16[8,240,128]{2,1,0:T(8,128)(2,1)}), bf16[8,240,128]{2,1,0:T(8,128)(2,1)S(1)}, u32[]{:S(2)}, u32[]{:S(2)}) async-start(bf16[8,240,128]{2,1,0:T(8,128)(2,1)} %attn.2), calls=%async_computation.2 | async-start | bytes 983040 | tf_op jit(solution)/shard_map/all_to_all | solution.py:294
  114.9 13.3 %collective-permute-start.17 = (bf16[48,480]{1,0:T(8,128)(2,1)S(1)}, bf16[48,480]{1,0:T(8,128)(2,1)S(1)}, u32[]{:S(2)}, u32[]{:S(2)}) collective-permute-start(bf16[48,480]{1,0:T(8,128)(2,1)S(1)} %get-tuple-element.229), channel_id=1, source_target_pairs={{0,6},{1,7},{2,0},{3,1},{4,2},{5,3},{6,4},{7,5},{8,14},{9,15},{10,... | collective-permute-start | bytes 138248 | tf_op jit(solution)/shard_map/ppermute | solution.py:381
  115.4 12.8 %collective-permute-start.16 = (bf16[48,480]{1,0:T(8,128)(2,1)S(1)}, bf16[48,480]{1,0:T(8,128)(2,1)S(1)}, u32[]{:S(2)}, u32[]{:S(2)}) collective-permute-start(bf16[48,480]{1,0:T(8,128)(2,1)S(1)} %get-tuple-element.230), channel_id=1, source_target_pairs={{0,4},{1,5},{2,6},{3,7},{4,0},{5,1},{6,2},{7,3},{8,12},{9,13},{10,... | collective-permute-start | bytes 138248 | tf_op jit(solution)/shard_map/ppermute | solution.py:381
  118.0 10.2 %collective-permute-start.15 = (bf16[48,480]{1,0:T(8,128)(2,1)S(1)}, bf16[48,480]{1,0:T(8,128)(2,1)S(1)}, u32[]{:S(2)}, u32[]{:S(2)}) collective-permute-start(bf16[48,480]{1,0:T(8,128)(2,1)S(1)} %get-tuple-element.228), channel_id=1, source_target_pairs={{0,2},{1,3},{2,4},{3,5},{4,6},{5,7},{6,0},{7,1},{8,10},{9,11},{10,... | collective-permute-start | bytes 138248 | tf_op jit(solution)/shard_map/ppermute | solution.py:381
  122.2 6.8 %collective-permute-start.11 = (bf16[112,128]{1,0:T(8,128)(2,1)}, bf16[112,128]{1,0:T(8,128)(2,1)S(1)}, u32[]{:S(2)}, u32[]{:S(2)}) collective-permute-start(bf16[112,128]{1,0:T(8,128)(2,1)} %get-tuple-element.159), channel_id=1, source_target_pairs={{0,64},{64,128},{128,192},{192,0},{1,65},{65,129},{129,193},{193,1... | collective-permute-start | bytes 86024 | tf_op jit(solution)/shard_map/ppermute | solution.py:298
  122.7 7.8 %collective-permute-start.12 = (bf16[112,128]{1,0:T(8,128)(2,1)}, bf16[112,128]{1,0:T(8,128)(2,1)S(1)}, u32[]{:S(2)}, u32[]{:S(2)}) collective-permute-start(bf16[112,128]{1,0:T(8,128)(2,1)} %get-tuple-element.160), channel_id=1, source_target_pairs={{0,128},{64,192},{128,0},{192,64},{1,129},{65,193},{129,1},{193,65... | collective-permute-start | bytes 86024 | tf_op jit(solution)/shard_map/ppermute | solution.py:298
  128.2 4.1 %collective-permute-start.13 = (bf16[112,128]{1,0:T(8,128)(2,1)}, bf16[112,128]{1,0:T(8,128)(2,1)S(1)}, u32[]{:S(2)}, u32[]{:S(2)}) collective-permute-start(bf16[112,128]{1,0:T(8,128)(2,1)} %get-tuple-element.161), channel_id=1, source_target_pairs={{0,192},{64,0},{128,64},{192,128},{1,193},{65,1},{129,65},{193,129... | collective-permute-start | bytes 86024 | tf_op jit(solution)/shard_map/ppermute | solution.py:298
  (10 other events, 39.9 us)

commit v2 on v1

--- a/solution.py
+++ b/solution.py
@@ -18,7 +18,7 @@
 LOG2E = math.log2(math.e)
 norm_eps = 1e-06
 VMEM = 56 << 20
-SIZES = (640, 1024)
+SIZES = (512, 768, 1024, 1152)
 
 HIST = ("x", "z")
 
@@ -115,7 +115,7 @@
             here = slice(g * group, (g + 1) * group)
             old = m_ref[here, :]
             new = jnp.maximum(old, jnp.max(s, axis=1, keepdims=True) * c2)
-            p = jnp.exp2(s * c2 - new[:, :1]).astype(jnp.bfloat16)
+            p = jnp.exp2(s * c2 - jnp.concatenate([new] * (count // 128), axis=1)).astype(jnp.bfloat16)
             r = dot(p, v, ((1,), (0,)))
             a = jnp.exp2(old - new)
             acc_ref[here, :] = acc_ref[here, :] * a + r[:, :128]
@@ -124,7 +124,7 @@
             s = later
 
     low = 0
-    for size in SIZES + (rows,):
+    for size in SIZES + (-(-rows // 128) * 128,):
         pl.when((limit > low) & (limit <= size))(functools.partial(step, low, size))
         low = size
 
@@ -151,7 +151,7 @@
     q_copy = pltpu.make_async_copy(q_ref.at[:, pl.ds(first, slots * part), :], q_buf, q_sem)
     q_copy.start()
     for u, ref in enumerate(kv_refs):
-        pltpu.make_async_copy(ref, kv.at[u], kv_sems.at[u]).start()
+        pltpu.make_async_copy(ref, kv.at[u, pl.ds(0, rows + 16), :], kv_sems.at[u]).start()
     acc_ref[...] = jnp.zeros_like(acc_ref)
     l_ref[...] = jnp.zeros_like(l_ref)
     m_ref[...] = jnp.full_like(m_ref, NEG)
@@ -159,7 +159,7 @@
     many = NZ // 2
 
     def kv_copy(u):
-        return pltpu.make_async_copy(kv_refs[0], kv.at[u], kv_sems.at[u])
+        return pltpu.make_async_copy(kv_refs[0], kv.at[u, pl.ds(0, rows + 16), :], kv_sems.at[u])
 
     row = lax.broadcasted_iota(jnp.int32, (16, 128), 0)
     for u, c in enumerate(small):
@@ -224,14 +224,14 @@
         out_specs=vmem,
         scratch_shapes=[
             pltpu.VMEM((NZ, slots * part, 128), jnp.bfloat16),
-            pltpu.VMEM((len(kvs), rows + 16, 256), jnp.bfloat16),
+            pltpu.VMEM((len(kvs), -(-rows // 128) * 128, 256), jnp.bfloat16),
             pltpu.VMEM((len(kvs), 16, 256), jnp.bfloat16),
             pltpu.SMEM((len(kvs),), jnp.int32),
         ]
         + [pltpu.VMEM((slots, NZ * part, 128), jnp.float32)] * 3
         + [pltpu.SemaphoreType.DMA] + [pltpu.SemaphoreType.DMA((len(kvs),))] * 2,
         compiler_params=pltpu.CompilerParams(vmem_limit_bytes=VMEM),
-        cost_estimate=cost(8 * slots, 1 << 20),
+        cost_estimate=cost(0.1 if slots == NX - 1 else 16, 1 << 10),
         name="attn",
     )(bounds, queries, *kvs)
 
@@ -311,10 +311,8 @@
     order = jnp.concatenate([order.reshape(NX * part, 128), last], axis=0)
     order, _ = lax.optimization_barrier((order, cache[0]))
     everyone = exchange(jnp.broadcast_to(order[None], (NZ,) + order.shape), "z")
-    last, kvs, terms, everyone = lax.optimization_barrier(
-        (cache[NX], kvs, conv(cache[0]), everyone)
-    )
-    lasts = [last] + [along_x(last, d) for d in range(1, NX)]
+    lasts = [cache[NX]] + [along_x(cache[NX], d) for d in range(1, NX)]
+    kvs, terms, everyone = lax.optimization_barrier((kvs, conv(cache[0]), everyone))
 
     landed = exchange(attn(bounds, everyone, kvs, part, c2), "z")
     landed_own = exchange(attn(bounds, everyone, kvs + lasts, part, c2), "z")

time: 138 us -> 135 us (0.978); the launches traced: 136 us -> 136 us
  starting transfers between devices: 50.6 us -> 47.5 us
  local copies, waits for them, and re-layouts: 11.2 us -> 13.5 us
    all_to_all x4, waiting for transfers between devices: 11.1 us -> 18.6 us  [exchange(): return lax.all_to_all(value, axis, 0, 0)]
    ppermute x9, waiting for transfers between devices: 7.15 us -> 0.02 us  [along_x(): return lax.ppermute(value, 'x', [(x, (x + dx) % NX) for x in range(NX)])]
    ppermute x9, starting transfers between devices: 15.6 us -> 12 us  [along_x(): return lax.ppermute(value, 'x', [(x, (x + dx) % NX) for x in range(NX)])]
    unnamed x27 -> x23, local copies, waits for them, and re-layouts: 2.76 us -> 3.19 us
  transfers between devices with their start and end apart: 22 -> 22, of which waited for: 9 -> 6; matrix products, arithmetic and copies ran while one was open for 10% -> 11% of each run, Pallas kernels for 28% -> 30%
where the time goes in v2:
time: 135 us; the launch traced here: 136 us
  starting transfers between devices  47.5 us (35%)
  Pallas kernels  42.9 us (32%)
  waiting for transfers between devices  26.2 us (19%)
  local copies, waits for them, and re-layouts  13.5 us (10%)
  matrix products  2.85 us (2%)
  between operations  1.5 us (1%)
    pallas_call x2, Pallas kernels, attn(): pl.pallas_call(functools.partial(attn_kernel, slots, part, rows, c2), out...  32.5 us
    all_to_all x4, starting transfers between devices, exchange(): return lax.all_to_all(value, axis, 0, 0)  22.2 us
    all_to_all x4, waiting for transfers between devices, exchange(): return lax.all_to_all(value, axis, 0, 0)  18.6 us
    ppermute x9, starting transfers between devices, along_x(): return lax.ppermute(value, 'x', [(x, (x + dx) % NX) for x in range(NX)])  12 us
    ppermute x3, waiting for transfers between devices, conv_terms(): squares = squares + lax.ppermute(squares, 'head', head_swap(bit))  7.59 us
    ppermute x3, starting transfers between devices, conv_sum(): lax.ppermute(piece, 'head', head_shift(d, 0)).astype(jnp.float32)  5 us
    pallas_call x1, Pallas kernels, pack_cache(): pl.pallas_call(pack_cache_kernel, in_specs=[smem, vmem, vmem], out_shape=...  4.38 us
    ppermute x1, starting transfers between devices, neighbour_rows(): low = lax.ppermute(latent[:, :, -1:], HIST, forward)  3.83 us
  transfers between devices with their start and end apart: 22, of which 6 were waited for; matrix products, arithmetic and copies ran while one was open for 11% of the time, Pallas kernels for 30%

profile of v2, /device:TPU:8, one launch (start us, length us, event | category | flops | bytes accessed | tf_op | source)
XLA Modules:
  0.0 135.8 jit_solution(4675439514594440027)
XLA Ops:
  1.7 3.8 %collective-permute-start.6 = (bf16[48,3,1,160]{0,3,2,1:T(8,128)(2,1)S(1)}, bf16[48,3,1,160]{0,3,2,1:T(8,128)(2,1)S(1)}, u32[]{:S(2)}, u32[]{:S(2)}) collective-permute-start(bf16[48,3,1,160]{0,3,2,1:T(8,128)(2,1)S(1)} %copy.19), channel_id=1, source_target_pairs={{0,8},{8,16},{16,24},{24,32},{32,40},{40,48},{48,56},{56,64},{64,7... | collective-permute-start | bytes 138248 | tf_op jit(solution)/shard_map/ppermute | solution.py:362
  8.6 8.9 %all-to-all-start = ((bf16[4,112,128]{2,1,0:T(8,128)(2,1)}), bf16[4,112,128]{2,1,0:T(8,128)(2,1)S(1)}, u32[]{:S(2)}, u32[]{:S(2)}) async-start(bf16[4,112,128]{2,1,0:T(8,128)(2,1)} %get-tuple-element.140), calls=%async_computation | async-start | bytes 229376 | tf_op jit(solution)/shard_map/all_to_all | solution.py:294
  18.1 4.4 %pack_kv.1 = (bf16[1360,256]{1,0:T(8,128)(2,1)}, bf16[1360,256]{1,0:T(8,128)(2,1)}, bf16[1360,256]{1,0:T(8,128)(2,1)}, bf16[1360,256]{1,0:T(8,128)(2,1)}, bf16[1360,256]{1,0:T(8,128)(2,1)}) custom-call(s32[1]{0:T(128)S(6)} %copy.27.len_ref, bf16[1344,640]{1,0:T(8,128)(2,1)} %k_ref, bf16[1344,640]{1,0:T(8,128)(2,1)} %v_ref), custom_call_target="tpu_custom_call" | custom-call | flops 3300000000 | bytes 7340032 | tf_op jit(solution)/shard_map/pack_kv/pallas_call | solution.py:88
  22.5 2.0 %collective-permute-start.3 = (bf16[1360,256]{1,0:T(8,128)(2,1)}, bf16[1360,256]{1,0:T(8,128)(2,1)}, u32[]{:S(2)}, u32[]{:S(2)}) collective-permute-start(bf16[1360,256]{1,0:T(8,128)(2,1)} %get-tuple-element.144), channel_id=1, source_target_pairs={{0,64},{64,128},{128,192},{192,0},{1,65},{65,129},{129,193},{193,1... | collective-permute-start | bytes 2088968 | tf_op jit(solution)/shard_map/ppermute | solution.py:298
  24.5 2.7 %collective-permute-start.4 = (bf16[1360,256]{1,0:T(8,128)(2,1)}, bf16[1360,256]{1,0:T(8,128)(2,1)}, u32[]{:S(2)}, u32[]{:S(2)}) collective-permute-start(bf16[1360,256]{1,0:T(8,128)(2,1)} %get-tuple-element.145), channel_id=1, source_target_pairs={{0,128},{64,192},{128,0},{192,64},{1,129},{65,193},{129,1},{193,65... | collective-permute-start | bytes 2088968 | tf_op jit(solution)/shard_map/ppermute | solution.py:298
  28.7 6.0 %all-to-all-start.1 = ((bf16[8,560,128]{2,1,0:T(8,128)(2,1)}), bf16[8,560,128]{2,1,0:T(8,128)(2,1)}, u32[]{:S(2)}, u32[]{:S(2)}) async-start(bf16[8,560,128]{2,1,0:T(8,128)(2,1)} %broadcast_in_dim.5), calls=%async_computation.1 | async-start | bytes 2293760 | tf_op jit(solution)/shard_map/all_to_all | solution.py:294
  37.1 20.2 %while.22 = (s32[]{:T(128)}, bf16[48,3,1,160]{0,3,2,1:T(8,128)(2,1)S(1)}, bf16[48,3,3,160]{0,3,2,1:T(8,128)(2,1)S(1)}, bf16[48,3,1,160]{0,3,2,1:T(8,128)(2,1)S(1...) while((s32[]{:T(128)}, ...), condition=%wide.region_2.3_spmd, body=%wide.region_0.2_spmd.sunk | while | flops 479679360 | bytes 10202133 | solution.py:330
  39.4 3.4 %collective-permute-done.1 = f32[3,5,160]{2,1,0:T(8,128)S(1)} collective-permute-done((f32[3,5,160]{2,1,0:T(8,128)S(1)}, f32[3,5,160]{2,1,0:T(8,128)S(1)}, u32[]{:S(2)}, u32[]{:S(2)}) %collective-permute-start.1) | collective-permute-done | bytes 9632 | tf_op jit(solution)/shard_map/while/body/ppermute | solution.py:338
  42.8 2.3 %collective-permute-start.2 = (f32[3,5,160]{2,1,0:T(8,128)S(1)}, f32[3,5,160]{2,1,0:T(8,128)S(1)}, u32[]{:S(2)}, u32[]{:S(2)}) collective-permute-start(f32[3,5,160]{2,1,0:T(8,128)S(1)} %add.168), channel_id=1, source_target_pairs={{0,4},{1,5},{2,6},{3,7},{4,0},{5,1},{6,2},{7,3},{8,12},{9,13},{10,... | collective-permute-start | bytes 28808 | tf_op jit(solution)/shard_map/while/body/ppermute | solution.py:338
  45.1 3.0 %collective-permute-done.2 = f32[3,5,160]{2,1,0:T(8,128)S(1)} collective-permute-done((f32[3,5,160]{2,1,0:T(8,128)S(1)}, f32[3,5,160]{2,1,0:T(8,128)S(1)}, u32[]{:S(2)}, u32[]{:S(2)}) %collective-permute-start.2) | collective-permute-done | bytes 9632 | tf_op jit(solution)/shard_map/while/body/ppermute | solution.py:338
  50.8 3.7 %concatenate.21 = bf16[1296,3,160]{0,2,1:T(8,128)(2,1)S(1)} concatenate(bf16[48,3,160]{0,2,1:T(8,128)(2,1)} %get-tuple-element.310, bf16[48,3,160]{0,2,1:T(8,128)(2,1)} %get-tuple-element.311, bf16[48,3,160]{0,2,1:T(8,128)(2,1)} %get-tuple-element.312, bf16[48,3,160]{0,2,1:T(8,128)(2,1)} %get-tuple-element.313, bf16[48,3,160]{0,2,1:T(8,128)(2,1)} %get-tuple-element.314, ...), dimensions={0} | concatenate | bytes 2488320 | tf_op jit(solution)/shard_map/while/body/concatenate | solution.py:352
  54.4 2.9 %convolution_convert_fusion.2 = bf16[3,160,384]{2,1,0:T(8,128)(2,1)} fusion(bf16[1296,3,160]{0,2,1:T(8,128)(2,1)S(1)} %concatenate.21, bf16[1296,384,1]{1,0,2:T(8,128)(2,1)} %bitcast.104), kind=kOutput, calls=%fused_computation.2.clone.1 | convolution fusion | flops 477941760 | bytes 2608128 | tf_op jit(solution)/shard_map/while/body/kyx,ko->oyx/dot_general | solution.py:354
  57.3 1.9 %collective-permute-start.8 = (bf16[1360,256]{1,0:T(8,128)(2,1)}, bf16[1360,256]{1,0:T(8,128)(2,1)S(1)}, u32[]{:S(2)}, u32[]{:S(2)}) collective-permute-start(bf16[1360,256]{1,0:T(8,128)(2,1)} %get-tuple-element.156.refs_4_), channel_id=1, source_target_pairs={{0,64},{64,128},{128,192},{192,0},{1,65},{65,129},{129,193},{193,1... | collective-permute-start | bytes 2088968 | tf_op jit(solution)/shard_map/ppermute | solution.py:298
  59.8 4.1 %all-to-all-done.1.q_ref = bf16[8,560,128]{2,1,0:T(8,128)(2,1)} async-done(((bf16[8,560,128]{2,1,0:T(8,128)(2,1)}), bf16[8,560,128]{2,1,0:T(8,128)(2,1)}, u32[]{:S(2)}, u32[]{:S(2)}) %all-to-all-start.1) | async-done | bytes 1146912 | tf_op jit(solution)/shard_map/all_to_all | solution.py:294
  65.4 21.7 %attn.3 = bf16[8,352,128]{2,1,0:T(8,128)(2,1)} custom-call(s32[4]{0:T(128)} %bounds_ref.3, bf16[8,560,128]{2,1,0:T(8,128)(2,1)} %all-to-all-done.1.q_ref, bf16[1360,256]{1,0:T(8,128)(2,1)} %get-tuple-element.152.refs_0_, bf16[1360,256]{1,0:T(8,128)(2,1)} %collective-permute-done.3.refs_1_, bf16[1360,256]{1,0:T(8,128)(2,1)} %collective-permute-done.4.refs_2_, ...), custom_call_target="tpu_custom_call" | custom-call | flops 110000000 | bytes 1024 | tf_op jit(solution)/shard_map/attn/pallas_call | solution.py:220
  87.1 3.8 %all-to-all-start.3 = ((bf16[8,352,128]{2,1,0:T(8,128)(2,1)}), bf16[8,352,128]{2,1,0:T(8,128)(2,1)S(1)}, u32[]{:S(2)}, u32[]{:S(2)}) async-start(bf16[8,352,128]{2,1,0:T(8,128)(2,1)} %attn.3), calls=%async_computation.3 | async-start | bytes 1441792 | tf_op jit(solution)/shard_map/all_to_all | solution.py:294
  91.8 10.8 %attn.2 = bf16[8,240,128]{2,1,0:T(8,128)(2,1)} custom-call(s32[4]{0:T(128)} %bounds_ref.3, bf16[8,560,128]{2,1,0:T(8,128)(2,1)} %all-to-all-done.1.q_ref, bf16[1360,256]{1,0:T(8,128)(2,1)} %get-tuple-element.152.refs_0_, bf16[1360,256]{1,0:T(8,128)(2,1)} %collective-permute-done.3.refs_1_, bf16[1360,256]{1,0:T(8,128)(2,1)} %collective-permute-done.4.refs_2_, ...), custom_call_target="tpu_custom_call" | custom-call | flops 17600000000 | bytes 1024 | tf_op jit(solution)/shard_map/attn/pallas_call | solution.py:220
  102.6 8.9 %all-to-all-done.3.ref = bf16[8,352,128]{2,1,0:T(8,128)(2,1)S(1)} async-done(((bf16[8,352,128]{2,1,0:T(8,128)(2,1)}), bf16[8,352,128]{2,1,0:T(8,128)(2,1)S(1)}, u32[]{:S(2)}, u32[]{:S(2)}) %all-to-all-start.3) | async-done | bytes 720928 | tf_op jit(solution)/shard_map/all_to_all | solution.py:294
  111.5 3.6 %all-to-all-start.2 = ((bf16[8,240,128]{2,1,0:T(8,128)(2,1)}), bf16[8,240,128]{2,1,0:T(8,128)(2,1)S(1)}, u32[]{:S(2)}, u32[]{:S(2)}) async-start(bf16[8,240,128]{2,1,0:T(8,128)(2,1)} %attn.2), calls=%async_computation.2 | async-start | bytes 983040 | tf_op jit(solution)/shard_map/all_to_all | solution.py:294
  117.9 2.4 %collective-permute-start.17 = (bf16[48,480]{1,0:T(8,128)(2,1)S(1)}, bf16[48,480]{1,0:T(8,128)(2,1)S(1)}, u32[]{:S(2)}, u32[]{:S(2)}) collective-permute-start(bf16[48,480]{1,0:T(8,128)(2,1)S(1)} %get-tuple-element.227), channel_id=1, source_target_pairs={{0,6},{1,7},{2,0},{3,1},{4,2},{5,3},{6,4},{7,5},{8,14},{9,15},{10,... | collective-permute-start | bytes 138248 | tf_op jit(solution)/shard_map/ppermute | solution.py:379
  120.3 2.3 %merge.1 = (bf16[112,128]{1,0:T(8,128)(2,1)}, bf16[112,128]{1,0:T(8,128)(2,1)}, bf16[112,128]{1,0:T(8,128)(2,1)}) custom-call(bf16[8,352,128]{2,1,0:T(8,128)(2,1)} %copy-done), custom_call_target="tpu_custom_call" | custom-call | flops 2200000000 | bytes 1048576 | tf_op jit(solution)/shard_map/merge/pallas_call | solution.py:266
  122.7 3.1 %collective-permute-start.13 = (bf16[112,128]{1,0:T(8,128)(2,1)}, bf16[112,128]{1,0:T(8,128)(2,1)S(1)}, u32[]{:S(2)}, u32[]{:S(2)}) collective-permute-start(bf16[112,128]{1,0:T(8,128)(2,1)} %get-tuple-element.159), channel_id=1, source_target_pairs={{0,192},{64,0},{128,64},{192,128},{1,193},{65,1},{129,65},{193,129... | collective-permute-start | bytes 86024 | tf_op jit(solution)/shard_map/ppermute | solution.py:298
  126.7 5.5 %all-to-all-done.2.ref = bf16[8,240,128]{2,1,0:T(8,128)(2,1)S(1)} async-done(((bf16[8,240,128]{2,1,0:T(8,128)(2,1)}), bf16[8,240,128]{2,1,0:T(8,128)(2,1)S(1)}, u32[]{:S(2)}, u32[]{:S(2)}) %all-to-all-start.2) | async-done | bytes 491552 | tf_op jit(solution)/shard_map/all_to_all | solution.py:294
  133.6 2.2 %finish.1 = bf16[112,640]{1,0:T(8,128)(2,1)} custom-call(bf16[8,240,128]{2,1,0:T(8,128)(2,1)} %copy-done.2, bf16[112,128]{1,0:T(8,128)(2,1)} %copy-done.7, bf16[112,128]{1,0:T(8,128)(2,1)} %copy-done.8, bf16[112,128]{1,0:T(8,128)(2,1)} %copy-done.9), custom_call_target="tpu_custom_call" | custom-call | flops 2200000000 | bytes 1048576 | tf_op jit(solution)/shard_map/finish/pallas_call | solution.py:285
  (72 shorter events, 20.9 us)
Async XLA Ops:
  1.7 34.4 %collective-permute-start.6 = (bf16[48,3,1,160]{0,3,2,1:T(8,128)(2,1)S(1)}, bf16[48,3,1,160]{0,3,2,1:T(8,128)(2,1)S(1)}, u32[]{:S(2)}, u32[]{:S(2)}) collective-permute-start(bf16[48,3,1,160]{0,3,2,1:T(8,128)(2,1)S(1)} %copy.19), channel_id=1, source_target_pairs={{0,8},{8,16},{16,24},{24,32},{32,40},{40,48},{48,56},{56,64},{64,7... | collective-permute-start | bytes 138248 | tf_op jit(solution)/shard_map/ppermute | solution.py:362
  5.7 30.5 %collective-permute-start.7 = (bf16[48,3,1,160]{0,3,2,1:T(8,128)(2,1)S(1)}, bf16[48,3,1,160]{0,3,2,1:T(8,128)(2,1)S(1)}, u32[]{:S(2)}, u32[]{:S(2)}) collective-permute-start(bf16[48,3,1,160]{0,3,2,1:T(8,128)(2,1)S(1)} %copy.20), channel_id=1, source_target_pairs={{8,0},{16,8},{24,16},{32,24},{40,32},{48,40},{56,48},{64,56},{72,6... | collective-permute-start | bytes 138248 | tf_op jit(solution)/shard_map/ppermute | solution.py:363
  8.6 18.9 %all-to-all-start = ((bf16[4,112,128]{2,1,0:T(8,128)(2,1)}), bf16[4,112,128]{2,1,0:T(8,128)(2,1)S(1)}, u32[]{:S(2)}, u32[]{:S(2)}) async-start(bf16[4,112,128]{2,1,0:T(8,128)(2,1)} %get-tuple-element.140), calls=%async_computation | async-start | bytes 229376 | tf_op jit(solution)/shard_map/all_to_all | solution.py:294
  18.1 9.1 %copy-start.1 = (bf16[48,3,3,160]{3,0,2,1:T(8,128)(2,1)S(1)}, bf16[48,3,3,160]{3,0,2,1:T(8,128)(2,1)}, u32[]{:S(2)}) copy-start(bf16[48,3,3,160]{3,0,2,1:T(8,128)(2,1)} %param.16) | copy-start | bytes 414724
  18.1 9.4 %copy-start.3 = (bf16[112,128]{1,0:T(8,128)(2,1)S(1)}, bf16[112,128]{1,0:T(8,128)(2,1)}, u32[]{:S(2)}) copy-start(bf16[112,128]{1,0:T(8,128)(2,1)} %get-tuple-element.149) | copy-start | bytes 86020
  22.5 36.7 %collective-permute-start.3 = (bf16[1360,256]{1,0:T(8,128)(2,1)}, bf16[1360,256]{1,0:T(8,128)(2,1)}, u32[]{:S(2)}, u32[]{:S(2)}) collective-permute-start(bf16[1360,256]{1,0:T(8,128)(2,1)} %get-tuple-element.144), channel_id=1, source_target_pairs={{0,64},{64,128},{128,192},{192,0},{1,65},{65,129},{129,193},{193,1... | collective-permute-start | bytes 2088968 | tf_op jit(solution)/shard_map/ppermute | solution.py:298
  24.5 35.3 %collective-permute-start.4 = (bf16[1360,256]{1,0:T(8,128)(2,1)}, bf16[1360,256]{1,0:T(8,128)(2,1)}, u32[]{:S(2)}, u32[]{:S(2)}) collective-permute-start(bf16[1360,256]{1,0:T(8,128)(2,1)} %get-tuple-element.145), channel_id=1, source_target_pairs={{0,128},{64,192},{128,0},{192,64},{1,129},{65,193},{129,1},{193,65... | collective-permute-start | bytes 2088968 | tf_op jit(solution)/shard_map/ppermute | solution.py:298
  28.7 35.2 %all-to-all-start.1 = ((bf16[8,560,128]{2,1,0:T(8,128)(2,1)}), bf16[8,560,128]{2,1,0:T(8,128)(2,1)}, u32[]{:S(2)}, u32[]{:S(2)}) async-start(bf16[8,560,128]{2,1,0:T(8,128)(2,1)} %broadcast_in_dim.5), calls=%async_computation.1 | async-start | bytes 2293760 | tf_op jit(solution)/shard_map/all_to_all | solution.py:294
  34.7 25.2 %collective-permute-start.5 = (bf16[1360,256]{1,0:T(8,128)(2,1)}, bf16[1360,256]{1,0:T(8,128)(2,1)}, u32[]{:S(2)}, u32[]{:S(2)}) collective-permute-start(bf16[1360,256]{1,0:T(8,128)(2,1)} %get-tuple-element.146), channel_id=1, source_target_pairs={{0,192},{64,0},{128,64},{192,128},{1,193},{65,1},{129,65},{193,129... | collective-permute-start | bytes 2088968 | tf_op jit(solution)/shard_map/ppermute | solution.py:298
  36.2 54.8 %collective-permute-start.10 = (bf16[1360,256]{1,0:T(8,128)(2,1)}, bf16[1360,256]{1,0:T(8,128)(2,1)}, u32[]{:S(2)}, u32[]{:S(2)}) collective-permute-start(bf16[1360,256]{1,0:T(8,128)(2,1)} %get-tuple-element.156.refs_4_), channel_id=1, source_target_pairs={{0,192},{64,0},{128,64},{192,128},{1,193},{65,1},{129,65},{193,129... | collective-permute-start | bytes 2088968 | tf_op jit(solution)/shard_map/ppermute | solution.py:298
  37.6 1.3 collective-permute-start
  38.9 3.8 %collective-permute-start.1 = (f32[3,5,160]{2,1,0:T(8,128)S(1)}, f32[3,5,160]{2,1,0:T(8,128)S(1)}, u32[]{:S(2)}, u32[]{:S(2)}) collective-permute-start(f32[3,5,160]{2,1,0:T(8,128)S(1)} %add.167), channel_id=1, source_target_pairs={{0,2},{1,3},{2,0},{3,1},{4,6},{5,7},{6,4},{7,5},{8,10},{9,11},{10,... | collective-permute-start | bytes 28808 | tf_op jit(solution)/shard_map/while/body/ppermute | solution.py:338
  42.8 5.3 %collective-permute-start.2 = (f32[3,5,160]{2,1,0:T(8,128)S(1)}, f32[3,5,160]{2,1,0:T(8,128)S(1)}, u32[]{:S(2)}, u32[]{:S(2)}) collective-permute-start(f32[3,5,160]{2,1,0:T(8,128)S(1)} %add.168), channel_id=1, source_target_pairs={{0,4},{1,5},{2,6},{3,7},{4,0},{5,1},{6,2},{7,3},{8,12},{9,13},{10,... | collective-permute-start | bytes 28808 | tf_op jit(solution)/shard_map/while/body/ppermute | solution.py:338
  57.3 33.7 %collective-permute-start.8 = (bf16[1360,256]{1,0:T(8,128)(2,1)}, bf16[1360,256]{1,0:T(8,128)(2,1)S(1)}, u32[]{:S(2)}, u32[]{:S(2)}) collective-permute-start(bf16[1360,256]{1,0:T(8,128)(2,1)} %get-tuple-element.156.refs_4_), channel_id=1, source_target_pairs={{0,64},{64,128},{128,192},{192,0},{1,65},{65,129},{129,193},{193,1... | collective-permute-start | bytes 2088968 | tf_op jit(solution)/shard_map/ppermute | solution.py:298
  59.2 31.7 %collective-permute-start.9 = (bf16[1360,256]{1,0:T(8,128)(2,1)}, bf16[1360,256]{1,0:T(8,128)(2,1)}, u32[]{:S(2)}, u32[]{:S(2)}) collective-permute-start(bf16[1360,256]{1,0:T(8,128)(2,1)} %get-tuple-element.156.refs_4_), channel_id=1, source_target_pairs={{0,128},{64,192},{128,0},{192,64},{1,129},{65,193},{129,1},{193,65... | collective-permute-start | bytes 2088968 | tf_op jit(solution)/shard_map/ppermute | solution.py:298
  65.1 50.0 %collective-permute-start.14 = (bf16[4,48,480]{2,1,0:T(8,128)(2,1)S(1)}, bf16[4,48,480]{2,1,0:T(8,128)(2,1)S(1)}, u32[]{:S(2)}, u32[]{:S(2)}) collective-permute-start(bf16[4,48,480]{2,1,0:T(8,128)(2,1)S(1)} %dynamic-slice_bitcast_fusion), channel_id=1, source_target_pairs={{0,1},{1,0},{2,3},{3,2},{4,5},{5,4},{6,7},{7,6},{8,9},{9,8},{10,11... | collective-permute-start | bytes 552968 | tf_op jit(solution)/shard_map/ppermute | solution.py:373
  87.1 24.4 %all-to-all-start.3 = ((bf16[8,352,128]{2,1,0:T(8,128)(2,1)}), bf16[8,352,128]{2,1,0:T(8,128)(2,1)S(1)}, u32[]{:S(2)}, u32[]{:S(2)}) async-start(bf16[8,352,128]{2,1,0:T(8,128)(2,1)} %attn.3), calls=%async_computation.3 | async-start | bytes 1441792 | tf_op jit(solution)/shard_map/all_to_all | solution.py:294
  111.5 20.7 %all-to-all-start.2 = ((bf16[8,240,128]{2,1,0:T(8,128)(2,1)}), bf16[8,240,128]{2,1,0:T(8,128)(2,1)S(1)}, u32[]{:S(2)}, u32[]{:S(2)}) async-start(bf16[8,240,128]{2,1,0:T(8,128)(2,1)} %attn.2), calls=%async_computation.2 | async-start | bytes 983040 | tf_op jit(solution)/shard_map/all_to_all | solution.py:294
  115.3 7.4 %collective-permute-start.15 = (bf16[48,480]{1,0:T(8,128)(2,1)S(1)}, bf16[48,480]{1,0:T(8,128)(2,1)S(1)}, u32[]{:S(2)}, u32[]{:S(2)}) collective-permute-start(bf16[48,480]{1,0:T(8,128)(2,1)S(1)} %get-tuple-element.226), channel_id=1, source_target_pairs={{0,2},{1,3},{2,4},{3,5},{4,6},{5,7},{6,0},{7,1},{8,10},{9,11},{10,... | collective-permute-start | bytes 138248 | tf_op jit(solution)/shard_map/ppermute | solution.py:379
  116.9 8.9 %collective-permute-start.16 = (bf16[48,480]{1,0:T(8,128)(2,1)S(1)}, bf16[48,480]{1,0:T(8,128)(2,1)S(1)}, u32[]{:S(2)}, u32[]{:S(2)}) collective-permute-start(bf16[48,480]{1,0:T(8,128)(2,1)S(1)} %get-tuple-element.228), channel_id=1, source_target_pairs={{0,4},{1,5},{2,6},{3,7},{4,0},{5,1},{6,2},{7,3},{8,12},{9,13},{10,... | collective-permute-start | bytes 138248 | tf_op jit(solution)/shard_map/ppermute | solution.py:379
  117.9 8.0 %collective-permute-start.17 = (bf16[48,480]{1,0:T(8,128)(2,1)S(1)}, bf16[48,480]{1,0:T(8,128)(2,1)S(1)}, u32[]{:S(2)}, u32[]{:S(2)}) collective-permute-start(bf16[48,480]{1,0:T(8,128)(2,1)S(1)} %get-tuple-element.227), channel_id=1, source_target_pairs={{0,6},{1,7},{2,0},{3,1},{4,2},{5,3},{6,4},{7,5},{8,14},{9,15},{10,... | collective-permute-start | bytes 138248 | tf_op jit(solution)/shard_map/ppermute | solution.py:379
  122.6 9.6 %collective-permute-start.11 = (bf16[112,128]{1,0:T(8,128)(2,1)}, bf16[112,128]{1,0:T(8,128)(2,1)S(1)}, u32[]{:S(2)}, u32[]{:S(2)}) collective-permute-start(bf16[112,128]{1,0:T(8,128)(2,1)} %get-tuple-element.157), channel_id=1, source_target_pairs={{0,64},{64,128},{128,192},{192,0},{1,65},{65,129},{129,193},{193,1... | collective-permute-start | bytes 86024 | tf_op jit(solution)/shard_map/ppermute | solution.py:298
  122.6 9.6 %collective-permute-start.12 = (bf16[112,128]{1,0:T(8,128)(2,1)}, bf16[112,128]{1,0:T(8,128)(2,1)S(1)}, u32[]{:S(2)}, u32[]{:S(2)}) collective-permute-start(bf16[112,128]{1,0:T(8,128)(2,1)} %get-tuple-element.158), channel_id=1, source_target_pairs={{0,128},{64,192},{128,0},{192,64},{1,129},{65,193},{129,1},{193,65... | collective-permute-start | bytes 86024 | tf_op jit(solution)/shard_map/ppermute | solution.py:298
  122.7 9.5 %collective-permute-start.13 = (bf16[112,128]{1,0:T(8,128)(2,1)}, bf16[112,128]{1,0:T(8,128)(2,1)S(1)}, u32[]{:S(2)}, u32[]{:S(2)}) collective-permute-start(bf16[112,128]{1,0:T(8,128)(2,1)} %get-tuple-element.159), channel_id=1, source_target_pairs={{0,192},{64,0},{128,64},{192,128},{1,193},{65,1},{129,65},{193,129... | collective-permute-start | bytes 86024 | tf_op jit(solution)/shard_map/ppermute | solution.py:298
  (8 other events, 28.9 us)
